TPU v7x, 32 devices: a whole 2x2x4 slice. The times are simulated.
32 devices in a mesh: sec: 8 (over z, core), term: 4 (over y, x).
Axes of the slice: x: 2, y: 2, z: 4, core: 2. Of those that a mesh axis runs over, the one named last changes fastest.
Arguments:
- psi: bfloat16 [32, 4, 256, 256], P('sec'), may hold values from -6 to 6
- left_env: bfloat16 [16, 32, 256, 256], P('term', 'sec'), may hold values from -0.09375 to 0.09375
- right_env: bfloat16 [16, 256, 256], P('term'), may hold values from -0.375 to 0.375
- site_ops: float32 [16, 4, 4], P('term'), may hold values from -3 to 3
- coupling: int32 [16, 32], P('term', 'sec'), may hold values from -1 to 31, as said below
- live: int32 [32], P('sec'), may hold values from 128 to 256, as said below
Outputs:
- sigma: bfloat16 [32, 4, 256, 256], P('sec', None, 'term')
Inputs may be any that keep to these rules, and one draw needn't show every extreme that they name: coupling[t, s] is -1 or a block within 2 of s; some terms couple at distance 2 in both directions. live sizes are at least 128.
All inputs are finite; a program needn't handle non-finite values.
Results may differ from a plain program's by a relative error of at most 0.018.
Values may be sent and summed in bfloat16 or wider, within the bound.
No kernel may reach another device: no remote copies, remote signals or barrier semaphores. Data moves between devices by JAX's collectives and lax.ppermute only.
A program may use at most 64 MiB of HBM per device.

v0:
```python
import jax
import jax.numpy as jnp
from jax import lax
from jax.sharding import PartitionSpec as P


def with_halo(value, sides, width):
    for axis, dim in sides:
        devices, length = (lax.axis_size(axis), value.shape[dim])
        up = [(i, (i + 1) % devices) for i in range(devices - 1)]
        down = [(j, i) for i, j in up]
        last = lax.slice_in_dim(value, length - width, length, axis=dim)
        first = lax.slice_in_dim(value, 0, width, axis=dim)
        before = lax.ppermute(last, axis, up)
        after = lax.ppermute(first, axis, down)
        value = jnp.concatenate([before, value, after], axis=dim)
    return value


def on_device(psi, left_env, right_env, site_ops, coupling, live):
    sec_count = psi.shape[0]
    width = psi.shape[2]
    row_count = width // lax.axis_size("term")
    row_start = lax.axis_index("term") * row_count
    extended = with_halo(psi, (("sec", 0),), 2)
    sec_base = lax.axis_index("sec") * sec_count

    def term_step(acc, inputs):
        left_t, right_t, ops_t, couple_t = inputs
        valid = couple_t >= 0
        index = jnp.where(valid, couple_t - sec_base + 2, 0)
        source = extended[index]
        mixed = jnp.einsum("kj,sjab->skab", ops_t, source.astype(jnp.float32))
        mixed = (mixed * valid[:, None, None, None].astype(jnp.float32)).astype(jnp.bfloat16)
        inner = jnp.einsum(
            "sab,skbc->skac", left_t, mixed, preferred_element_type=jnp.float32
        ).astype(jnp.bfloat16)
        outer = jnp.einsum("skac,cd->skad", inner, right_t, preferred_element_type=jnp.float32)
        return (acc + outer, None)

    start = jnp.zeros(psi.shape, jnp.float32)
    total, unused = lax.scan(term_step, start, (left_env, right_env, site_ops, coupling))
    mine = lax.psum_scatter(total, "term", scatter_dimension=2, tiled=True)
    rows_here = row_start + jnp.arange(row_count, dtype=jnp.int32)
    columns = jnp.arange(width, dtype=jnp.int32)
    rows_ok = rows_here[None, :] < live[:, None]
    cols_ok = columns[None, :] < live[:, None]
    keep = rows_ok[:, :, None] & cols_ok[:, None, :]
    result = jnp.where(keep[:, None, :, :], mine, 0.0)
    return result.astype(jnp.bfloat16)


def solution(mesh):
    placed = (
        P("sec", None, None, None),
        P("term", "sec", None, None),
        P("term", None, None),
        P("term", None, None),
        P("term", "sec"),
        P("sec"),
    )
    return jax.shard_map(
        on_device,
        mesh=mesh,
        in_specs=placed,
        out_specs=P("sec", None, "term", None),
        check_vma=False,
    )
```

profile of v0, /device:TPU:0, one launch (start us, length us, event | category | flops | bytes accessed | tf_op | source)
XLA Modules:
  0.0 149.8 jit_solution(16095885689748807119)
XLA Ops:
  6.5 2.8 %fusion.27 = (bf16[2,4,256,256]{3,2,1,0:T(8,128)(2,1)}, bf16[2,4,256,256]{3,2,1,0:T(8,128)(2,1)S(1)}) fusion(bf16[4,4,256,256]{3,2,1,0:T(8,128)(2,1)} %param.8), kind=kLoop, calls=%fused_computation.33 | loop fusion | bytes 4194304 | tf_op jit(solution)/shard_map/slice | solution.py:12
  9.4 3.3 %collective-permute-start = (bf16[2,4,256,256]{3,2,1,0:T(8,128)(2,1)}, bf16[2,4,256,256]{3,2,1,0:T(8,128)(2,1)}, u32[]{:S(2)}, u32[]{:S(2)}) collective-permute-start(bf16[2,4,256,256]{3,2,1,0:T(8,128)(2,1)} %get-tuple-element.91), channel_id=1, source_target_pairs={{0,4},{4,8},{8,12},{12,16},{16,20},{20,24},{24,28},{1,5},{5,9},{9,... | collective-permute-start | bytes 3145736 | tf_op jit(solution)/shard_map/ppermute | solution.py:14
  12.7 1.3 collective-permute-start.1
  14.0 0.3 collective-permute-done
  14.3 4.3 %collective-permute-done.1 = bf16[2,4,256,256]{3,2,1,0:T(8,128)(2,1)} collective-permute-done((bf16[2,4,256,256]{3,2,1,0:T(8,128)(2,1)S(1)}, bf16[2,4,256,256]{3,2,1,0:T(8,128)(2,1)}, u32[]{:S(2)}, u32[]{:S(2)}) %collective-permute-start.1) | collective-permute-done | bytes 1048608 | tf_op jit(solution)/shard_map/ppermute | solution.py:15
  18.6 3.4 %pad_maximum_fusion = bf16[8,4,256,256]{3,2,1,0:T(8,128)(2,1)} fusion(bf16[2,4,256,256]{3,2,1,0:T(8,128)(2,1)} %collective-permute-done.1, bf16[4,4,256,256]{3,2,1,0:T(8,128)(2,1)S(1)} %copy-done, bf16[2,4,256,256]{3,2,1,0:T(8,128)(2,1)} %collective-permute-done), kind=kLoop, calls=%fused_computation.27 | loop fusion | flops 4194304 | bytes 8388608 | tf_op jit(solution)/shard_map/concatenate | solution.py:16
  22.0 54.0 %while.11 = (s32[]{:T(128)}, f32[4,4,256,256]{3,2,1,0:T(8,128)}, s32[4,4]{1,0:T(4,128)S(1)}, s32[]{:T(128)}, bf16[8,4,256,256]{3,2,1,0:T(8,128)(2,1)}, /*index=5...) while((s32[]{:T(128)}, f32[4,4,256,256]{3,2,1,0:T(8,128)}, ...), condition=%wide.region_1.2_spmd.clone, body=%wide.region_0.1_spmd.clone.sunk | while | flops 1087374336 | bytes 23730416 | solution.py:42
  22.0 2.9 %gather_fusion = bf16[4,4,256,256]{3,2,1,0:T(8,128)(2,1)S(1)} fusion(bf16[8,4,256,256]{3,2,1,0:T(8,128)(2,1)} %get-tuple-element.166, s32[1024]{0:T(1024)S(1)} %pad_clamp_fusion.2), kind=kCustom, calls=%fused_computation.clone.clone.1 | custom fusion | bytes 4194320 | tf_op jit(solution)/shard_map/while/body/eval_jaxpr/gather | solution.py:32
  24.9 3.7 %fusion.44 = f32[4,256,256,4]{2,3,1,0:T(4,128)} fusion(bf16[4,4,256,256]{3,2,1,0:T(8,128)(2,1)S(1)} %gather_fusion, bf16[4,4,4]{2,1,0:T(4,128)(2,1)S(1)} %get-tuple-element.167, s32[]{:T(128)} %get-tuple-element.152), kind=kOutput, calls=%fused_computation.7.clone.1 | convolution fusion | flops 8388608 | bytes 6292484 | tf_op jit(solution)/shard_map/while/body/eval_jaxpr/kj,sjab->skab/dot_general | solution.py:33
  28.6 5.9 %select_add_fusion.2 = f32[4,4,256,256]{3,2,1,0:T(8,128)} fusion(f32[4,4,256,256]{3,2,1,0:T(8,128)} %get-tuple-element.153, pred[]{:T(512)S(6)} %compare.3, f32[4,256,256,4]{2,3,1,0:T(4,128)} %fusion.44, f32[4]{0:T(128)S(1)} %fusion.45, bf16[4,4,256,256]{3,2,1,0:T(8,128)(2,1)} %get-tuple-element.168, s32[]{:T(128)} %get-tuple-element.152, ...), kind=kOutput, calls=%fused_computation.3.clone.1 | convolution fusion | flops 1078984704 | bytes 13239313 | tf_op jit(solution)/shard_map/while/body/eval_jaxpr/skac,cd->skad/dot_general | solution.py:38
  34.5 2.9 %gather_fusion = bf16[4,4,256,256]{3,2,1,0:T(8,128)(2,1)S(1)} fusion(bf16[8,4,256,256]{3,2,1,0:T(8,128)(2,1)} %get-tuple-element.166, s32[1024]{0:T(1024)S(1)} %pad_clamp_fusion.2), kind=kCustom, calls=%fused_computation.clone.clone.1 | custom fusion | bytes 4194320 | tf_op jit(solution)/shard_map/while/body/eval_jaxpr/gather | solution.py:32
  37.4 3.7 %fusion.44 = f32[4,256,256,4]{2,3,1,0:T(4,128)} fusion(bf16[4,4,256,256]{3,2,1,0:T(8,128)(2,1)S(1)} %gather_fusion, bf16[4,4,4]{2,1,0:T(4,128)(2,1)S(1)} %get-tuple-element.167, s32[]{:T(128)} %get-tuple-element.152), kind=kOutput, calls=%fused_computation.7.clone.1 | convolution fusion | flops 8388608 | bytes 6292484 | tf_op jit(solution)/shard_map/while/body/eval_jaxpr/kj,sjab->skab/dot_general | solution.py:33
  41.1 7.2 %select_add_fusion.2 = f32[4,4,256,256]{3,2,1,0:T(8,128)} fusion(f32[4,4,256,256]{3,2,1,0:T(8,128)} %get-tuple-element.153, pred[]{:T(512)S(6)} %compare.3, f32[4,256,256,4]{2,3,1,0:T(4,128)} %fusion.44, f32[4]{0:T(128)S(1)} %fusion.45, bf16[4,4,256,256]{3,2,1,0:T(8,128)(2,1)} %get-tuple-element.168, s32[]{:T(128)} %get-tuple-element.152, ...), kind=kOutput, calls=%fused_computation.3.clone.1 | convolution fusion | flops 1078984704 | bytes 13239313 | tf_op jit(solution)/shard_map/while/body/eval_jaxpr/skac,cd->skad/dot_general | solution.py:38
  48.3 2.9 %gather_fusion = bf16[4,4,256,256]{3,2,1,0:T(8,128)(2,1)S(1)} fusion(bf16[8,4,256,256]{3,2,1,0:T(8,128)(2,1)} %get-tuple-element.166, s32[1024]{0:T(1024)S(1)} %pad_clamp_fusion.2), kind=kCustom, calls=%fused_computation.clone.clone.1 | custom fusion | bytes 4194320 | tf_op jit(solution)/shard_map/while/body/eval_jaxpr/gather | solution.py:32
  51.2 3.7 %fusion.44 = f32[4,256,256,4]{2,3,1,0:T(4,128)} fusion(bf16[4,4,256,256]{3,2,1,0:T(8,128)(2,1)S(1)} %gather_fusion, bf16[4,4,4]{2,1,0:T(4,128)(2,1)S(1)} %get-tuple-element.167, s32[]{:T(128)} %get-tuple-element.152), kind=kOutput, calls=%fused_computation.7.clone.1 | convolution fusion | flops 8388608 | bytes 6292484 | tf_op jit(solution)/shard_map/while/body/eval_jaxpr/kj,sjab->skab/dot_general | solution.py:33
  54.9 7.3 %select_add_fusion.2 = f32[4,4,256,256]{3,2,1,0:T(8,128)} fusion(f32[4,4,256,256]{3,2,1,0:T(8,128)} %get-tuple-element.153, pred[]{:T(512)S(6)} %compare.3, f32[4,256,256,4]{2,3,1,0:T(4,128)} %fusion.44, f32[4]{0:T(128)S(1)} %fusion.45, bf16[4,4,256,256]{3,2,1,0:T(8,128)(2,1)} %get-tuple-element.168, s32[]{:T(128)} %get-tuple-element.152, ...), kind=kOutput, calls=%fused_computation.3.clone.1 | convolution fusion | flops 1078984704 | bytes 13239313 | tf_op jit(solution)/shard_map/while/body/eval_jaxpr/skac,cd->skad/dot_general | solution.py:38
  62.2 2.9 %gather_fusion = bf16[4,4,256,256]{3,2,1,0:T(8,128)(2,1)S(1)} fusion(bf16[8,4,256,256]{3,2,1,0:T(8,128)(2,1)} %get-tuple-element.166, s32[1024]{0:T(1024)S(1)} %pad_clamp_fusion.2), kind=kCustom, calls=%fused_computation.clone.clone.1 | custom fusion | bytes 4194320 | tf_op jit(solution)/shard_map/while/body/eval_jaxpr/gather | solution.py:32
  65.0 3.7 %fusion.44 = f32[4,256,256,4]{2,3,1,0:T(4,128)} fusion(bf16[4,4,256,256]{3,2,1,0:T(8,128)(2,1)S(1)} %gather_fusion, bf16[4,4,4]{2,1,0:T(4,128)(2,1)S(1)} %get-tuple-element.167, s32[]{:T(128)} %get-tuple-element.152), kind=kOutput, calls=%fused_computation.7.clone.1 | convolution fusion | flops 8388608 | bytes 6292484 | tf_op jit(solution)/shard_map/while/body/eval_jaxpr/kj,sjab->skab/dot_general | solution.py:33
  68.7 7.2 %select_add_fusion.2 = f32[4,4,256,256]{3,2,1,0:T(8,128)} fusion(f32[4,4,256,256]{3,2,1,0:T(8,128)} %get-tuple-element.153, pred[]{:T(512)S(6)} %compare.3, f32[4,256,256,4]{2,3,1,0:T(4,128)} %fusion.44, f32[4]{0:T(128)S(1)} %fusion.45, bf16[4,4,256,256]{3,2,1,0:T(8,128)(2,1)} %get-tuple-element.168, s32[]{:T(128)} %get-tuple-element.152, ...), kind=kOutput, calls=%fused_computation.3.clone.1 | convolution fusion | flops 1078984704 | bytes 13239313 | tf_op jit(solution)/shard_map/while/body/eval_jaxpr/skac,cd->skad/dot_general | solution.py:38
  76.0 0.6 copy-done.3
  76.6 0.1 iota_compare_fusion
  76.8 0.1 broadcast_and_fusion
  76.9 63.9 %reduce-scatter.2.cloned.1.call-done = f32[4,4,64,256]{3,2,1,0:T(8,128)} async-done(((f32[4,4,256,256]{3,2,1,0:T(8,128)}), f32[4,4,64,256]{3,2,1,0:T(8,128)}) %reduce-scatter.2.cloned.1.call-update) | async-done | bytes 1048592 | tf_op jit(solution)/shard_map/reduce_scatter | solution.py:43
  140.8 2.1 %select_convert_fusion = bf16[4,4,64,256]{3,2,1,0:T(8,128)(2,1)} fusion(f32[4,4,64,256]{3,2,1,0:T(8,128)} %reduce-scatter.2.cloned.1.call-done, pred[4,64,256]{2,1,0:T(8,128)(4,1)S(1)} %broadcast_and_fusion), kind=kLoop, calls=%fused_computation.28 | loop fusion | flops 262144 | bytes 1638400 | tf_op jit(solution)/shard_map/convert_element_type | solution.py:50
  (25 shorter events, 0.2 us)
Async XLA Ops:
  6.5 12.1 %copy-start = (bf16[4,4,256,256]{3,2,1,0:T(8,128)(2,1)S(1)}, bf16[4,4,256,256]{3,2,1,0:T(8,128)(2,1)}, u32[]{:S(2)}) copy-start(bf16[4,4,256,256]{3,2,1,0:T(8,128)(2,1)} %param.8) | copy-start | bytes 6291460
  6.5 7.5 %copy-start.1 = (f32[4,4,4]{2,1,0:T(4,128)S(1)}, f32[4,4,4]{2,1,0:T(4,128)}, u32[]{:S(2)}) copy-start(f32[4,4,4]{2,1,0:T(4,128)} %param.11) | copy-start | bytes 772
  6.5 134.3 %reduce-scatter.2.cloned.1.call-start = ((), (), s32[]{:S(2)}) async-start(), calls=%async_computation.1 | async-start | bytes 5242880 | tf_op jit(solution)/shard_map/reduce_scatter | solution.py:43
  9.4 5.0 %collective-permute-start = (bf16[2,4,256,256]{3,2,1,0:T(8,128)(2,1)}, bf16[2,4,256,256]{3,2,1,0:T(8,128)(2,1)}, u32[]{:S(2)}, u32[]{:S(2)}) collective-permute-start(bf16[2,4,256,256]{3,2,1,0:T(8,128)(2,1)} %get-tuple-element.91), channel_id=1, source_target_pairs={{0,4},{4,8},{8,12},{12,16},{16,20},{20,24},{24,28},{1,5},{5,9},{9,... | collective-permute-start | bytes 3145736 | tf_op jit(solution)/shard_map/ppermute | solution.py:14
  12.7 5.9 %collective-permute-start.1 = (bf16[2,4,256,256]{3,2,1,0:T(8,128)(2,1)S(1)}, bf16[2,4,256,256]{3,2,1,0:T(8,128)(2,1)}, u32[]{:S(2)}, u32[]{:S(2)}) collective-permute-start(bf16[2,4,256,256]{3,2,1,0:T(8,128)(2,1)S(1)} %get-tuple-element.92), channel_id=1, source_target_pairs={{4,0},{8,4},{12,8},{16,12},{20,16},{24,20},{28,24},{5,1},{9,5},{13... | collective-permute-start | bytes 3145736 | tf_op jit(solution)/shard_map/ppermute | solution.py:15
  14.0 8.0 %copy-start.2 = (s32[4,4]{1,0:T(4,128)S(1)}, s32[4,4]{1,0:T(4,128)}, u32[]{:S(2)}) copy-start(s32[4,4]{1,0:T(4,128)} %param.12) | copy-start | bytes 196
  76.0 0.7 copy-start.3
Sparse Core Ops, SparseCore 0:
  76.1 64.6 reduce-scatter.1
where the time goes:
time: 150 us
  waiting for transfers between devices  68.5 us (46%)
  matrix products  42.3 us (28%)
  local copies, waits for them, and re-layouts  14.9 us (10%)
  between operations  13.5 us (9%)
  other arithmetic  5.88 us (4%)
  starting transfers between devices  4.59 us (3%)
    reduce_scatter x1, waiting for transfers between devices, on_device(): mine = lax.psum_scatter(total, 'term', scatter_dimension=2, tiled=True)  63.9 us
    dot_general x4, matrix products, term_step(): jnp.einsum('skac,cd->skad', inner, right_t, preferred_element_type=jnp.fl...  27.7 us
    dot_general x4, matrix products, term_step(): mixed = jnp.einsum('kj,sjab->skab', ops_t, source.astype(jnp.float32))  14.7 us
    gather x4, local copies, waits for them, and re-layouts, term_step(): source = extended[index]  11.5 us
    ppermute x1, waiting for transfers between devices, with_halo(): after = lax.ppermute(first, axis, down)  4.27 us
    concatenate x1, other arithmetic, with_halo(): value = jnp.concatenate([before, value, after], axis=dim)  3.39 us
    ppermute x1, starting transfers between devices, with_halo(): before = lax.ppermute(last, axis, up)  3.31 us
  transfers between devices with their start and end apart: 3, of which 3 were waited for; matrix products, arithmetic and copies ran while one was open for 0% of the time, Pallas kernels for 0%

commit v1 on v0

v1 whole, which is shorter than its diff:
```python
import functools

import jax
import jax.numpy as jnp
from jax import lax
from jax.experimental import pallas as pl
from jax.experimental.pallas import tpu as pltpu
from jax.sharding import PartitionSpec as P

VMEM_LIMIT = 40 * 1024 * 1024


def flip(value, bit):
    size = lax.axis_size("term")
    return lax.ppermute(value, "term", [(i, i ^ bit) for i in range(size)])


def apply_body(firsts, facing, orders, info, couple, ops, psi, left, right, *refs):
    extras, rest = refs[: -(2 * len(orders) + 6)], refs[-(2 * len(orders) + 6) :]
    outs, (ext, lv, rv, mixed, inner, sems) = rest[: 2 * len(orders)], rest[2 * len(orders) :]
    terms, width = right.shape[0], right.shape[1]
    states = ops.shape[1]
    count = len(firsts[0])
    own = psi.shape[0]
    devices = len(orders[0])
    rows = width // devices
    base, odd, me = info[0], info[1], info[2]

    def block_of(n):
        return jnp.where(odd == 1, firsts[1][n], firsts[0][n])

    copies = [pltpu.make_async_copy(psi, ext.at[pl.ds(0, own)], sems.at[0])]
    at = own
    for extra in extras:
        copies.append(pltpu.make_async_copy(extra, ext.at[pl.ds(at, extra.shape[0])], sems.at[1 + at - own]))
        at += extra.shape[0]
    slots = at
    for n in range(count):
        for i in range(devices):
            copies.append(
                pltpu.make_async_copy(
                    left.at[:, block_of(n), pl.ds(pl.multiple_of((i ^ me) * rows, rows), rows), :],
                    lv.at[n, :, pl.ds(i * rows, rows), :],
                    sems.at[4 + n * devices + i],
                )
            )
    copies.append(pltpu.make_async_copy(right, rv, sems.at[3]))
    for copy in copies:
        copy.start()
    for copy in copies:
        copy.wait()

    for n in range(count):
        s = block_of(n)
        for t in range(terms):
            c = couple[t, s]
            valid = jnp.where(c >= 0, 1.0, 0.0).astype(jnp.float32)
            r = c - base
            if facing:
                other = jnp.where(odd == 1, r + own + 2, r)
            else:
                other = jnp.where(odd == 1, r, own - 1 - r)
            slot = jnp.where((r >= 0) & (r < own), r, other)
            slot = jnp.clip(jnp.where(c >= 0, slot, 0), 0, slots - 1)
            coef = [[ops[t, k, j] * valid for j in range(states)] for k in range(states)]
            for a in range(0, width, 16):
                source = [ext[slot, j, a : a + 16, :].astype(jnp.float32) for j in range(states)]
                for k in range(states):
                    value = coef[k][0] * source[0]
                    for j in range(1, states):
                        value = value + coef[k][j] * source[j]
                    mixed[t % 2, a : a + 16, k * width : (k + 1) * width] = value.astype(jnp.bfloat16)
            value = jnp.dot(lv[n, t], mixed[t % 2], preferred_element_type=jnp.float32)
            for k in range(states):
                inner[k * width : (k + 1) * width, t * width : (t + 1) * width] = value[
                    :, k * width : (k + 1) * width
                ].astype(jnp.bfloat16)
        for k in range(states):
            value = jnp.dot(
                inner[k * width : (k + 1) * width, :],
                rv[...].reshape(terms * width, width),
                preferred_element_type=jnp.float32,
            ).astype(jnp.bfloat16)
            path = k * len(orders) // states
            kk = k % (states // len(orders))
            keep, send = outs[2 * path], outs[2 * path + 1]
            half = devices // 2
            for at, i in enumerate(orders[path]):
                target = keep if at < half else send
                target[at % half, n, kk] = value[i * rows : (i + 1) * rows, :]


def apply_blocks(firsts, facing, orders, info, couple, ops, psi, left, right, extras):
    terms, width = right.shape[0], right.shape[1]
    states = ops.shape[1]
    count = len(firsts[0])
    devices = len(orders[0])
    rows = width // devices
    paths = len(orders)
    part = jax.ShapeDtypeStruct((devices // 2, count, states // paths, rows, width), jnp.bfloat16)
    smem = pl.BlockSpec(memory_space=pltpu.SMEM)
    hbm = pl.BlockSpec(memory_space=pl.ANY)
    vmem = pl.BlockSpec(memory_space=pltpu.VMEM)
    slots = psi.shape[0] + sum(e.shape[0] for e in extras)
    pairs = count * terms
    return pl.pallas_call(
        functools.partial(apply_body, firsts, facing, orders),
        out_shape=[part] * (2 * paths),
        in_specs=[smem] * 3 + [hbm] * (3 + len(extras)),
        out_specs=[vmem] * (2 * paths),
        scratch_shapes=[
            pltpu.VMEM((slots,) + psi.shape[1:], jnp.bfloat16),
            pltpu.VMEM((count, terms, width, width), jnp.bfloat16),
            pltpu.VMEM((terms, width, width), jnp.bfloat16),
            pltpu.VMEM((2, width, states * width), jnp.bfloat16),
            pltpu.VMEM((states * width, terms * width), jnp.bfloat16),
            pltpu.SemaphoreType.DMA((4 + count * devices,)),
        ],
        compiler_params=pltpu.CompilerParams(vmem_limit_bytes=VMEM_LIMIT),
        cost_estimate=pl.CostEstimate(
            flops=pairs * states * 4 * width**3, bytes_accessed=4 * 1024 * 1024, transcendentals=0
        ),
        name=f"apply_{'facing' if facing else 'outer'}_{count}",
    )(info, couple, ops, psi, left, right, *extras)


def finish_body(firsts, info, live, *refs):
    out = refs[-1]
    odd, me = info[1], info[2]
    rows, width = out.shape[2], out.shape[3]
    at = 0
    for group in firsts:
        count = len(group[0])
        for path in range(2):
            keep, first, last = refs[at : at + 3]
            at += 3
            kh = keep.shape[2]
            for n in range(count):
                s = jnp.where(odd == 1, group[1][n], group[0][n])
                size = live[s]
                row = lax.broadcasted_iota(jnp.int32, (rows, width), 0) + me * rows
                col = lax.broadcasted_iota(jnp.int32, (rows, width), 1)
                ok = (row < size) & (col < size)
                for kk in range(kh):
                    value = keep[0, n, kk].astype(jnp.float32) + first[0, n, kk].astype(jnp.float32)
                    value = value + last[0, n, kk].astype(jnp.float32)
                    out[s, path * kh + kk] = jnp.where(ok, value, 0.0).astype(jnp.bfloat16)


def finish(firsts, info, live, parts, shape):
    smem = pl.BlockSpec(memory_space=pltpu.SMEM)
    vmem = pl.BlockSpec(memory_space=pltpu.VMEM)
    return pl.pallas_call(
        functools.partial(finish_body, firsts),
        out_shape=jax.ShapeDtypeStruct(shape, jnp.bfloat16),
        in_specs=[smem] * 2 + [vmem] * len(parts),
        out_specs=vmem,
        compiler_params=pltpu.CompilerParams(vmem_limit_bytes=VMEM_LIMIT),
        name="finish",
    )(info, live, *parts)


def on_device(psi, left, right, ops, couple, live):
    secs, devices = lax.axis_size("sec"), lax.axis_size("term")
    sec, term = lax.axis_index("sec"), lax.axis_index("term")
    own, states, width = psi.shape[0], psi.shape[1], psi.shape[2]
    odd = sec % 2
    info = jnp.stack([sec * own, odd, term]).astype(jnp.int32)

    bits = [1 << b for b in range(devices.bit_length() - 1)]
    paths = (bits, bits[::-1])
    orders = tuple(
        tuple(sorted(range(devices), key=lambda i: [bool(i & b) for b in path])) for path in paths
    )

    chip = [(i, i ^ 1) for i in range(secs)]
    link = [(i, i + 1) for i in range(1, secs - 1, 2)]
    link = link + [(j, i) for i, j in link]
    facing_send = lax.dynamic_slice_in_dim(psi, (1 - odd) * 2, 2, 0)
    near_send = lax.dynamic_slice_in_dim(psi, odd * 3, 1, 0)
    far_send = lax.dynamic_slice_in_dim(psi, 1 + odd, 1, 0)
    inside = lax.ppermute(facing_send, "sec", chip)
    near = lax.ppermute(near_send, "sec", link)
    far = lax.ppermute(far_send, "sec", link)

    groups = (((2, 3), (0, 1)), ((1,), (2,)), ((0,), (3,)))
    extras = ((inside,), (near,), (near, far))
    parts = []
    for g, group in enumerate(groups):
        made = apply_blocks(group, g == 0, orders, info, couple, ops, psi, left, right, extras[g])
        for p, path in enumerate(paths):
            keep, send = made[2 * p], made[2 * p + 1]
            got = flip(send, path[0])
            for bit in path[1:-1]:
                half = keep.shape[0] // 2
                total = keep + got
                keep, send = total[:half], total[half:]
                got = flip(send, bit)
            send = keep[1:] + got[1:]
            parts += [keep[:1], got[:1], flip(send, path[-1])]
    shape = (own, states, width // devices, width)
    return finish(groups, info, live, parts, shape)


def solution(mesh):
    placed = (
        P("sec", None, None, None),
        P("term", "sec", None, None),
        P("term", None, None),
        P("term", None, None),
        P("term", "sec"),
        P("sec"),
    )
    return jax.shard_map(
        on_device,
        mesh=mesh,
        in_specs=placed,
        out_specs=P("sec", None, "term", None),
        check_vma=False,
    )
```

time: 150 us -> 53.9 us (0.36)
  the two profiles are of different devices: /device:TPU:0 before, /device:TPU:8 now
where the time goes in v1:
time: 53.9 us; the launch traced here: 53.7 us
  starting transfers between devices  17.6 us (33%)
  Pallas kernels  15.4 us (29%)
  waiting for transfers between devices  15.2 us (28%)
  local copies, waits for them, and re-layouts  5.1 us (9%)
    pallas_call x3, Pallas kernels, apply_blocks(): pl.pallas_call(functools.partial(apply_body, firsts, facing, orders), out...  13.8 us
    ppermute x12, starting transfers between devices, flip(): return lax.ppermute(value, 'term', [(i, i ^ bit) for i in range(size)])  12 us
    ppermute x12, waiting for transfers between devices, flip(): return lax.ppermute(value, 'term', [(i, i ^ bit) for i in range(size)])  10.2 us
    ppermute x1, waiting for transfers between devices, on_device(): near = lax.ppermute(near_send, 'sec', link)  5.05 us
    ppermute x1, starting transfers between devices, on_device(): far = lax.ppermute(far_send, 'sec', link)  3.64 us
    dynamic_slice x1, local copies, waits for them, and re-layouts, on_device(): facing_send = lax.dynamic_slice_in_dim(psi, (1 - odd) * 2, 2, 0)  2.43 us
    ppermute x1, starting transfers between devices, on_device(): near = lax.ppermute(near_send, 'sec', link)  1.91 us
    unnamed x12, local copies, waits for them, and re-layouts  1.61 us
  transfers between devices with their start and end apart: 15, of which 4 were waited for; matrix products, arithmetic and copies ran while one was open for 2% of the time, Pallas kernels for 26%

profile of v1, /device:TPU:8, one launch (start us, length us, event | category | flops | bytes accessed | tf_op | source)
XLA Modules:
  0.0 53.7 jit_solution(4903493524833875696)
XLA Ops:
  0.0 2.4 %constant_dynamic-slice_fusion.2 = bf16[2,4,256,256]{3,2,1,0:T(8,128)(2,1)} fusion(bf16[4,4,256,256]{3,2,1,0:T(8,128)(2,1)} %psi.5, s32[]{:T(128)S(6)} %select_n.17), kind=kLoop, calls=%fused_computation.8 | loop fusion | bytes 2097156 | tf_op jit(solution)/shard_map/dynamic_slice | solution.py:179
  2.5 1.1 %constant_dynamic-slice_fusion = (bf16[1,4,256,256]{3,2,1,0:T(8,128)(2,1)}, bf16[1,4,256,256]{3,2,1,0:T(8,128)(2,1)}) fusion(bf16[4,4,256,256]{3,2,1,0:T(8,128)(2,1)S(1)} %copy-done, s32[]{:T(128)S(6)} %select_n.19, s32[]{:T(128)S(6)} %select_n.18), kind=kLoop, calls=%fused_computation.6 | loop fusion | bytes 2097160 | tf_op jit(solution)/shard_map/dynamic_slice | solution.py:181
  3.5 1.9 %collective-permute-start.5 = (bf16[1,4,256,256]{3,2,1,0:T(8,128)(2,1)}, bf16[1,4,256,256]{3,2,1,0:T(8,128)(2,1)S(1)}, u32[]{:S(2)}, u32[]{:S(2)}) collective-permute-start(bf16[1,4,256,256]{3,2,1,0:T(8,128)(2,1)} %get-tuple-element.30), channel_id=1, source_target_pairs={{4,8},{12,16},{20,24},{8,4},{16,12},{24,20},{5,9},{13,17},{21,25},... | collective-permute-start | bytes 1572872 | tf_op jit(solution)/shard_map/ppermute | solution.py:183
  5.4 3.6 %collective-permute-start.10 = (bf16[1,4,256,256]{3,2,1,0:T(8,128)(2,1)}, bf16[1,4,256,256]{3,2,1,0:T(8,128)(2,1)}, u32[]{:S(2)}, u32[]{:S(2)}) collective-permute-start(bf16[1,4,256,256]{3,2,1,0:T(8,128)(2,1)} %get-tuple-element.29), channel_id=1, source_target_pairs={{4,8},{12,16},{20,24},{8,4},{16,12},{24,20},{5,9},{13,17},{21,25},... | collective-permute-start | bytes 1572872 | tf_op jit(solution)/shard_map/ppermute | solution.py:184
  9.2 5.0 %collective-permute-done.5.refs_0_ = bf16[1,4,256,256]{3,2,1,0:T(8,128)(2,1)S(1)} collective-permute-done((bf16[1,4,256,256]{3,2,1,0:T(8,128)(2,1)}, bf16[1,4,256,256]{3,2,1,0:T(8,128)(2,1)S(1)}, u32[]{:S(2)}, u32[]{:S(2)}) %collective-permute-start.5) | collective-permute-done | bytes 524320 | tf_op jit(solution)/shard_map/ppermute | solution.py:183
  14.2 1.6 %copy-done.1 = bf16[4,4,256,256]{3,2,1,0:T(8,128)(2,1)S(1)} copy-done((bf16[4,4,256,256]{3,2,1,0:T(8,128)(2,1)S(1)}, bf16[4,4,256,256]{3,2,1,0:T(8,128)(2,1)}, u32[]{:S(2)}) %copy-start.1) | copy-done | bytes 2097176
  15.8 3.3 %apply_outer_1.2 = (bf16[2,1,2,64,256]{4,3,2,1,0:T(8,128)(2,1)S(1)}, bf16[2,1,2,64,256]{4,3,2,1,0:T(8,128)(2,1)S(1)}, bf16[2,1,2,64,256]{4,3,2,1,0:T(8,128)(2,1)S(1)}, bf16[2,1,2,64,256]{4,3,2,1,0:T(8,128)(2,1)S(1)}) custom-call(s32[3]{0:T(128)S(1)} %pad_add_fusion.info, s32[4,4]{1,0:T(4,128)S(1)} %copy-done.4, f32[4,4,4]{2,1,0:T(4,128)S(1)} %copy-done.3, ...), custom_call_target="tpu_custom_call" | custom-call | flops 1073741824 | bytes 4194304 | tf_op jit(solution)/shard_map/apply_outer_1/pallas_call | solution.py:106
  19.2 1.6 %collective-permute-start.6 = (bf16[2,1,2,64,256]{4,3,2,1,0:T(8,128)(2,1)S(1)}, bf16[2,1,2,64,256]{4,3,2,1,0:T(8,128)(2,1)S(1)}, u32[]{:S(2)}, u32[]{:S(2)}) collective-permute-start(bf16[2,1,2,64,256]{4,3,2,1,0:T(8,128)(2,1)S(1)} %get-tuple-element.22), channel_id=1, source_target_pairs={{0,1},{1,0},{2,3},{3,2},{4,5},{5,4},{6,7},{7,6},{8,9},{9,8},{10,11... | collective-permute-start | bytes 393224 | tf_op jit(solution)/shard_map/ppermute | solution.py:15
  20.7 1.5 %collective-permute-start.8 = (bf16[2,1,2,64,256]{4,3,2,1,0:T(8,128)(2,1)S(1)}, bf16[2,1,2,64,256]{4,3,2,1,0:T(8,128)(2,1)S(1)}, u32[]{:S(2)}, u32[]{:S(2)}) collective-permute-start(bf16[2,1,2,64,256]{4,3,2,1,0:T(8,128)(2,1)S(1)} %get-tuple-element.24), channel_id=1, source_target_pairs={{0,2},{1,3},{2,0},{3,1},{4,6},{5,7},{6,4},{7,5},{8,10},{9,11},{10,... | collective-permute-start | bytes 393224 | tf_op jit(solution)/shard_map/ppermute | solution.py:15
  22.2 4.2 %apply_outer_1.3 = (bf16[2,1,2,64,256]{4,3,2,1,0:T(8,128)(2,1)S(1)}, bf16[2,1,2,64,256]{4,3,2,1,0:T(8,128)(2,1)S(1)}, bf16[2,1,2,64,256]{4,3,2,1,0:T(8,128)(2,1)S(1)}, bf16[2,1,2,64,256]{4,3,2,1,0:T(8,128)(2,1)S(1)}) custom-call(s32[3]{0:T(128)S(1)} %pad_add_fusion.info, s32[4,4]{1,0:T(4,128)S(1)} %copy-done.4, f32[4,4,4]{2,1,0:T(4,128)S(1)} %copy-done.3, ...), custom_call_target="tpu_custom_call" | custom-call | flops 1073741824 | bytes 4194304 | tf_op jit(solution)/shard_map/apply_outer_1/pallas_call | solution.py:106
  26.4 0.6 %collective-permute-start.11 = (bf16[2,1,2,64,256]{4,3,2,1,0:T(8,128)(2,1)S(1)}, bf16[2,1,2,64,256]{4,3,2,1,0:T(8,128)(2,1)S(1)}, u32[]{:S(2)}, u32[]{:S(2)}) collective-permute-start(bf16[2,1,2,64,256]{4,3,2,1,0:T(8,128)(2,1)S(1)} %get-tuple-element.26), channel_id=1, source_target_pairs={{0,1},{1,0},{2,3},{3,2},{4,5},{5,4},{6,7},{7,6},{8,9},{9,8},{10,11... | collective-permute-start | bytes 393224 | tf_op jit(solution)/shard_map/ppermute | solution.py:15
  27.0 0.5 collective-permute-start.13
  27.6 1.6 %collective-permute-start.7 = (bf16[1,1,2,64,256]{4,3,2,1,0:T(8,128)(2,1)S(1)}, bf16[1,1,2,64,256]{4,3,2,1,0:T(8,128)(2,1)S(1)}, u32[]{:S(2)}, u32[]{:S(2)}) collective-permute-start(bf16[1,1,2,64,256]{4,3,2,1,0:T(8,128)(2,1)S(1)} %get-tuple-element.46), channel_id=1, source_target_pairs={{0,2},{1,3},{2,0},{3,1},{4,6},{5,7},{6,4},{7,5},{8,10},{9,11},{10,... | collective-permute-start | bytes 196616 | tf_op jit(solution)/shard_map/ppermute | solution.py:15
  29.2 6.3 %apply_facing_2.1 = (bf16[2,2,2,64,256]{4,3,2,1,0:T(8,128)(2,1)S(1)}, bf16[2,2,2,64,256]{4,3,2,1,0:T(8,128)(2,1)S(1)}, bf16[2,2,2,64,256]{4,3,2,1,0:T(8,128)(2,1)S(1)}, bf16[2,2,2,64,256]{4,3,2,1,0:T(8,128)(2,1)S(1)}) custom-call(s32[3]{0:T(128)S(1)} %pad_add_fusion.info, s32[4,4]{1,0:T(4,128)S(1)} %copy-done.4, f32[4,4,4]{2,1,0:T(4,128)S(1)} %copy-done.3, ...), custom_call_target="tpu_custom_call" | custom-call | flops 2147483648 | bytes 4194304 | tf_op jit(solution)/shard_map/apply_facing_2/pallas_call | solution.py:106
  35.5 1.6 %collective-permute-start.1 = (bf16[2,2,2,64,256]{4,3,2,1,0:T(8,128)(2,1)S(1)}, bf16[2,2,2,64,256]{4,3,2,1,0:T(8,128)(2,1)S(1)}, u32[]{:S(2)}, u32[]{:S(2)}) collective-permute-start(bf16[2,2,2,64,256]{4,3,2,1,0:T(8,128)(2,1)S(1)} %get-tuple-element.18), channel_id=1, source_target_pairs={{0,1},{1,0},{2,3},{3,2},{4,5},{5,4},{6,7},{7,6},{8,9},{9,8},{10,11... | collective-permute-start | bytes 786440 | tf_op jit(solution)/shard_map/ppermute | solution.py:15
  37.1 0.6 %collective-permute-start.9 = (bf16[1,1,2,64,256]{4,3,2,1,0:T(8,128)(2,1)S(1)}, bf16[1,1,2,64,256]{4,3,2,1,0:T(8,128)(2,1)S(1)}, u32[]{:S(2)}, u32[]{:S(2)}) collective-permute-start(bf16[1,1,2,64,256]{4,3,2,1,0:T(8,128)(2,1)S(1)} %get-tuple-element.43), channel_id=1, source_target_pairs={{0,1},{1,0},{2,3},{3,2},{4,5},{5,4},{6,7},{7,6},{8,9},{9,8},{10,11... | collective-permute-start | bytes 196616 | tf_op jit(solution)/shard_map/ppermute | solution.py:15
  38.2 5.8 %collective-permute-done.1 = bf16[2,2,2,64,256]{4,3,2,1,0:T(8,128)(2,1)S(1)} collective-permute-done((bf16[2,2,2,64,256]{4,3,2,1,0:T(8,128)(2,1)S(1)}, bf16[2,2,2,64,256]{4,3,2,1,0:T(8,128)(2,1)S(1)}, u32[]{:S(2)}, u32[]{:S(2)}) %collective-permute-start.1) | collective-permute-done | bytes 262176 | tf_op jit(solution)/shard_map/ppermute | solution.py:15
  43.9 0.5 collective-permute-start.12
  44.5 0.7 %collective-permute-done.3 = bf16[2,2,2,64,256]{4,3,2,1,0:T(8,128)(2,1)S(1)} collective-permute-done((bf16[2,2,2,64,256]{4,3,2,1,0:T(8,128)(2,1)S(1)}, bf16[2,2,2,64,256]{4,3,2,1,0:T(8,128)(2,1)S(1)}, u32[]{:S(2)}, u32[]{:S(2)}) %collective-permute-start.3) | collective-permute-done | bytes 262176 | tf_op jit(solution)/shard_map/ppermute | solution.py:15
  45.2 0.9 %collective-permute-start.2 = (bf16[1,2,2,64,256]{4,3,2,1,0:T(8,128)(2,1)S(1)}, bf16[1,2,2,64,256]{4,3,2,1,0:T(8,128)(2,1)S(1)}, u32[]{:S(2)}, u32[]{:S(2)}) collective-permute-start(bf16[1,2,2,64,256]{4,3,2,1,0:T(8,128)(2,1)S(1)} %get-tuple-element.34), channel_id=1, source_target_pairs={{0,2},{1,3},{2,0},{3,1},{4,6},{5,7},{6,4},{7,5},{8,10},{9,11},{10,... | collective-permute-start | bytes 393224 | tf_op jit(solution)/shard_map/ppermute | solution.py:15
  46.1 1.6 %collective-permute-start.4 = (bf16[1,2,2,64,256]{4,3,2,1,0:T(8,128)(2,1)S(1)}, bf16[1,2,2,64,256]{4,3,2,1,0:T(8,128)(2,1)S(1)}, u32[]{:S(2)}, u32[]{:S(2)}) collective-permute-start(bf16[1,2,2,64,256]{4,3,2,1,0:T(8,128)(2,1)S(1)} %get-tuple-element.31), channel_id=1, source_target_pairs={{0,1},{1,0},{2,3},{3,2},{4,5},{5,4},{6,7},{7,6},{8,9},{9,8},{10,11... | collective-permute-start | bytes 393224 | tf_op jit(solution)/shard_map/ppermute | solution.py:15
  47.7 0.6 %collective-permute-start.14 = (bf16[1,1,2,64,256]{4,3,2,1,0:T(8,128)(2,1)S(1)}, bf16[1,1,2,64,256]{4,3,2,1,0:T(8,128)(2,1)S(1)}, u32[]{:S(2)}, u32[]{:S(2)}) collective-permute-start(bf16[1,1,2,64,256]{4,3,2,1,0:T(8,128)(2,1)S(1)} %get-tuple-element.37), channel_id=1, source_target_pairs={{0,1},{1,0},{2,3},{3,2},{4,5},{5,4},{6,7},{7,6},{8,9},{9,8},{10,11... | collective-permute-start | bytes 196616 | tf_op jit(solution)/shard_map/ppermute | solution.py:15
  48.3 3.7 %collective-permute-done.14.refs_17_ = bf16[1,1,2,64,256]{4,3,2,1,0:T(8,128)(2,1)S(1)} collective-permute-done((bf16[1,1,2,64,256]{4,3,2,1,0:T(8,128)(2,1)S(1)}, bf16[1,1,2,64,256]{4,3,2,1,0:T(8,128)(2,1)S(1)}, u32[]{:S(2)}, u32[]{:S(2)}) %collective-permute-start.14) | collective-permute-done | bytes 65568 | tf_op jit(solution)/shard_map/ppermute | solution.py:15
  52.1 1.6 %finish.1 = bf16[4,4,64,256]{3,2,1,0:T(8,128)(2,1)} custom-call(s32[3]{0:T(128)S(1)} %pad_add_fusion.info, s32[4]{0:T(128)S(1)} %copy-done.5, bf16[1,2,2,64,256]{4,3,2,1,0:T(8,128)(2,1)S(1)} %get-tuple-element.35.refs_0_, bf16[1,2,2,64,256]{4,3,2,1,0:T(8,128)(2,1)S(1)} %get-tuple-element.36.refs_1_, ...), custom_call_target="tpu_custom_call" | custom-call | tf_op jit(solution)/shard_map/finish/pallas_call | solution.py:153
  (31 shorter events, 0.8 us)
Async XLA Ops:
  0.0 2.5 %copy-start = (bf16[4,4,256,256]{3,2,1,0:T(8,128)(2,1)S(1)}, bf16[4,4,256,256]{3,2,1,0:T(8,128)(2,1)}, u32[]{:S(2)}) copy-start(bf16[4,4,256,256]{3,2,1,0:T(8,128)(2,1)} %psi.5) | copy-start | bytes 6291460
  0.0 14.2 %copy-start.2 = (bf16[4,256,256]{2,1,0:T(8,128)(2,1)S(1)}, bf16[4,256,256]{2,1,0:T(8,128)(2,1)}, u32[]{:S(2)}) copy-start(bf16[4,256,256]{2,1,0:T(8,128)(2,1)} %right.5) | copy-start | bytes 1572868
  0.0 14.2 %copy-start.3 = (f32[4,4,4]{2,1,0:T(4,128)S(1)}, f32[4,4,4]{2,1,0:T(4,128)}, u32[]{:S(2)}) copy-start(f32[4,4,4]{2,1,0:T(4,128)} %ops.5) | copy-start | bytes 772
  0.0 14.2 %copy-start.4 = (s32[4,4]{1,0:T(4,128)S(1)}, s32[4,4]{1,0:T(4,128)}, u32[]{:S(2)}) copy-start(s32[4,4]{1,0:T(4,128)} %couple.5) | copy-start | bytes 196
  2.5 26.7 %collective-permute-start = (bf16[2,4,256,256]{3,2,1,0:T(8,128)(2,1)}, bf16[2,4,256,256]{3,2,1,0:T(8,128)(2,1)}, u32[]{:S(2)}, u32[]{:S(2)}) collective-permute-start(bf16[2,4,256,256]{3,2,1,0:T(8,128)(2,1)} %constant_dynamic-slice_fusion.2), channel_id=1, source_target_pairs={{0,4},{4,0},{8,12},{12,8},{16,20},{20,16},{24,28},{28,24},{1,5},{5... | collective-permute-start | bytes 3145736 | tf_op jit(solution)/shard_map/ppermute | solution.py:182
  3.5 10.7 %collective-permute-start.5 = (bf16[1,4,256,256]{3,2,1,0:T(8,128)(2,1)}, bf16[1,4,256,256]{3,2,1,0:T(8,128)(2,1)S(1)}, u32[]{:S(2)}, u32[]{:S(2)}) collective-permute-start(bf16[1,4,256,256]{3,2,1,0:T(8,128)(2,1)} %get-tuple-element.30), channel_id=1, source_target_pairs={{4,8},{12,16},{20,24},{8,4},{16,12},{24,20},{5,9},{13,17},{21,25},... | collective-permute-start | bytes 1572872 | tf_op jit(solution)/shard_map/ppermute | solution.py:183
  5.4 16.8 %collective-permute-start.10 = (bf16[1,4,256,256]{3,2,1,0:T(8,128)(2,1)}, bf16[1,4,256,256]{3,2,1,0:T(8,128)(2,1)}, u32[]{:S(2)}, u32[]{:S(2)}) collective-permute-start(bf16[1,4,256,256]{3,2,1,0:T(8,128)(2,1)} %get-tuple-element.29), channel_id=1, source_target_pairs={{4,8},{12,16},{20,24},{8,4},{16,12},{24,20},{5,9},{13,17},{21,25},... | collective-permute-start | bytes 1572872 | tf_op jit(solution)/shard_map/ppermute | solution.py:184
  14.2 1.6 %copy-start.1 = (bf16[4,4,256,256]{3,2,1,0:T(8,128)(2,1)S(1)}, bf16[4,4,256,256]{3,2,1,0:T(8,128)(2,1)}, u32[]{:S(2)}) copy-start(bf16[4,4,256,256]{3,2,1,0:T(8,128)(2,1)} %left.5) | copy-start | bytes 6291460
  19.2 8.4 %collective-permute-start.6 = (bf16[2,1,2,64,256]{4,3,2,1,0:T(8,128)(2,1)S(1)}, bf16[2,1,2,64,256]{4,3,2,1,0:T(8,128)(2,1)S(1)}, u32[]{:S(2)}, u32[]{:S(2)}) collective-permute-start(bf16[2,1,2,64,256]{4,3,2,1,0:T(8,128)(2,1)S(1)} %get-tuple-element.22), channel_id=1, source_target_pairs={{0,1},{1,0},{2,3},{3,2},{4,5},{5,4},{6,7},{7,6},{8,9},{9,8},{10,11... | collective-permute-start | bytes 393224 | tf_op jit(solution)/shard_map/ppermute | solution.py:15
  20.7 16.3 %collective-permute-start.8 = (bf16[2,1,2,64,256]{4,3,2,1,0:T(8,128)(2,1)S(1)}, bf16[2,1,2,64,256]{4,3,2,1,0:T(8,128)(2,1)S(1)}, u32[]{:S(2)}, u32[]{:S(2)}) collective-permute-start(bf16[2,1,2,64,256]{4,3,2,1,0:T(8,128)(2,1)S(1)} %get-tuple-element.24), channel_id=1, source_target_pairs={{0,2},{1,3},{2,0},{3,1},{4,6},{5,7},{6,4},{7,5},{8,10},{9,11},{10,... | collective-permute-start | bytes 393224 | tf_op jit(solution)/shard_map/ppermute | solution.py:15
  26.4 11.3 %collective-permute-start.11 = (bf16[2,1,2,64,256]{4,3,2,1,0:T(8,128)(2,1)S(1)}, bf16[2,1,2,64,256]{4,3,2,1,0:T(8,128)(2,1)S(1)}, u32[]{:S(2)}, u32[]{:S(2)}) collective-permute-start(bf16[2,1,2,64,256]{4,3,2,1,0:T(8,128)(2,1)S(1)} %get-tuple-element.26), channel_id=1, source_target_pairs={{0,1},{1,0},{2,3},{3,2},{4,5},{5,4},{6,7},{7,6},{8,9},{9,8},{10,11... | collective-permute-start | bytes 393224 | tf_op jit(solution)/shard_map/ppermute | solution.py:15
  27.0 19.1 %collective-permute-start.13 = (bf16[2,1,2,64,256]{4,3,2,1,0:T(8,128)(2,1)S(1)}, bf16[2,1,2,64,256]{4,3,2,1,0:T(8,128)(2,1)S(1)}, u32[]{:S(2)}, u32[]{:S(2)}) collective-permute-start(bf16[2,1,2,64,256]{4,3,2,1,0:T(8,128)(2,1)S(1)} %get-tuple-element.28), channel_id=1, source_target_pairs={{0,2},{1,3},{2,0},{3,1},{4,6},{5,7},{6,4},{7,5},{8,10},{9,11},{10,... | collective-permute-start | bytes 393224 | tf_op jit(solution)/shard_map/ppermute | solution.py:15
  27.6 20.2 %collective-permute-start.7 = (bf16[1,1,2,64,256]{4,3,2,1,0:T(8,128)(2,1)S(1)}, bf16[1,1,2,64,256]{4,3,2,1,0:T(8,128)(2,1)S(1)}, u32[]{:S(2)}, u32[]{:S(2)}) collective-permute-start(bf16[1,1,2,64,256]{4,3,2,1,0:T(8,128)(2,1)S(1)} %get-tuple-element.46), channel_id=1, source_target_pairs={{0,2},{1,3},{2,0},{3,1},{4,6},{5,7},{6,4},{7,5},{8,10},{9,11},{10,... | collective-permute-start | bytes 196616 | tf_op jit(solution)/shard_map/ppermute | solution.py:15
  35.5 16.6 %copy-start.5 = (s32[4]{0:T(128)S(1)}, s32[4]{0:T(128)}, u32[]{:S(2)}) copy-start(s32[4]{0:T(128)} %live.1) | copy-start | bytes 52
  35.5 8.5 %collective-permute-start.1 = (bf16[2,2,2,64,256]{4,3,2,1,0:T(8,128)(2,1)S(1)}, bf16[2,2,2,64,256]{4,3,2,1,0:T(8,128)(2,1)S(1)}, u32[]{:S(2)}, u32[]{:S(2)}) collective-permute-start(bf16[2,2,2,64,256]{4,3,2,1,0:T(8,128)(2,1)S(1)} %get-tuple-element.18), channel_id=1, source_target_pairs={{0,1},{1,0},{2,3},{3,2},{4,5},{5,4},{6,7},{7,6},{8,9},{9,8},{10,11... | collective-permute-start | bytes 786440 | tf_op jit(solution)/shard_map/ppermute | solution.py:15
  37.1 11.3 %collective-permute-start.9 = (bf16[1,1,2,64,256]{4,3,2,1,0:T(8,128)(2,1)S(1)}, bf16[1,1,2,64,256]{4,3,2,1,0:T(8,128)(2,1)S(1)}, u32[]{:S(2)}, u32[]{:S(2)}) collective-permute-start(bf16[1,1,2,64,256]{4,3,2,1,0:T(8,128)(2,1)S(1)} %get-tuple-element.43), channel_id=1, source_target_pairs={{0,1},{1,0},{2,3},{3,2},{4,5},{5,4},{6,7},{7,6},{8,9},{9,8},{10,11... | collective-permute-start | bytes 196616 | tf_op jit(solution)/shard_map/ppermute | solution.py:15
  37.7 7.5 %collective-permute-start.3 = (bf16[2,2,2,64,256]{4,3,2,1,0:T(8,128)(2,1)S(1)}, bf16[2,2,2,64,256]{4,3,2,1,0:T(8,128)(2,1)S(1)}, u32[]{:S(2)}, u32[]{:S(2)}) collective-permute-start(bf16[2,2,2,64,256]{4,3,2,1,0:T(8,128)(2,1)S(1)} %get-tuple-element.20), channel_id=1, source_target_pairs={{0,2},{1,3},{2,0},{3,1},{4,6},{5,7},{6,4},{7,5},{8,10},{9,11},{10,... | collective-permute-start | bytes 786440 | tf_op jit(solution)/shard_map/ppermute | solution.py:15
  43.9 4.4 %collective-permute-start.12 = (bf16[1,1,2,64,256]{4,3,2,1,0:T(8,128)(2,1)S(1)}, bf16[1,1,2,64,256]{4,3,2,1,0:T(8,128)(2,1)S(1)}, u32[]{:S(2)}, u32[]{:S(2)}) collective-permute-start(bf16[1,1,2,64,256]{4,3,2,1,0:T(8,128)(2,1)S(1)} %get-tuple-element.40), channel_id=1, source_target_pairs={{0,2},{1,3},{2,0},{3,1},{4,6},{5,7},{6,4},{7,5},{8,10},{9,11},{10,... | collective-permute-start | bytes 196616 | tf_op jit(solution)/shard_map/ppermute | solution.py:15
  45.2 6.9 %collective-permute-start.2 = (bf16[1,2,2,64,256]{4,3,2,1,0:T(8,128)(2,1)S(1)}, bf16[1,2,2,64,256]{4,3,2,1,0:T(8,128)(2,1)S(1)}, u32[]{:S(2)}, u32[]{:S(2)}) collective-permute-start(bf16[1,2,2,64,256]{4,3,2,1,0:T(8,128)(2,1)S(1)} %get-tuple-element.34), channel_id=1, source_target_pairs={{0,2},{1,3},{2,0},{3,1},{4,6},{5,7},{6,4},{7,5},{8,10},{9,11},{10,... | collective-permute-start | bytes 393224 | tf_op jit(solution)/shard_map/ppermute | solution.py:15
  46.1 5.9 %collective-permute-start.4 = (bf16[1,2,2,64,256]{4,3,2,1,0:T(8,128)(2,1)S(1)}, bf16[1,2,2,64,256]{4,3,2,1,0:T(8,128)(2,1)S(1)}, u32[]{:S(2)}, u32[]{:S(2)}) collective-permute-start(bf16[1,2,2,64,256]{4,3,2,1,0:T(8,128)(2,1)S(1)} %get-tuple-element.31), channel_id=1, source_target_pairs={{0,1},{1,0},{2,3},{3,2},{4,5},{5,4},{6,7},{7,6},{8,9},{9,8},{10,11... | collective-permute-start | bytes 393224 | tf_op jit(solution)/shard_map/ppermute | solution.py:15
  47.7 4.3 %collective-permute-start.14 = (bf16[1,1,2,64,256]{4,3,2,1,0:T(8,128)(2,1)S(1)}, bf16[1,1,2,64,256]{4,3,2,1,0:T(8,128)(2,1)S(1)}, u32[]{:S(2)}, u32[]{:S(2)}) collective-permute-start(bf16[1,1,2,64,256]{4,3,2,1,0:T(8,128)(2,1)S(1)} %get-tuple-element.37), channel_id=1, source_target_pairs={{0,1},{1,0},{2,3},{3,2},{4,5},{5,4},{6,7},{7,6},{8,9},{9,8},{10,11... | collective-permute-start | bytes 196616 | tf_op jit(solution)/shard_map/ppermute | solution.py:15

commit v2 on v0

v2 whole, which is shorter than its diff:
```python
import functools

import jax
import jax.numpy as jnp
from jax import lax
from jax.experimental import pallas as pl
from jax.experimental.pallas import tpu as pltpu
from jax.sharding import PartitionSpec as P

VMEM_LIMIT = 24 * 1024 * 1024
COST = 10


def flip(value, routes, step):
    secs, devices = lax.axis_size("sec"), lax.axis_size("term")
    pairs = []
    for sec in range(secs):
        for term in range(devices):
            pairs.append((sec * devices + term, sec * devices + (term ^ routes[sec % 2][step])))
    return lax.ppermute(value, ("sec", "term"), pairs)


def over_link(value, bit):
    secs, devices = lax.axis_size("sec"), lax.axis_size("term")
    pairs = []
    for sec in range(secs):
        other = sec + 1 if sec % 2 else sec - 1
        for term in range(devices):
            to = other * devices + term if 0 <= other < secs else sec * devices + (term ^ bit)
            pairs.append((sec * devices + term, to))
    return lax.ppermute(value, ("sec", "term"), pairs)


def pick_body(psi, right, own, rv, *refs):
    outs, sems = refs[:-1], refs[-1]
    odd = lax.axis_index("sec") % 2
    copies = [pltpu.make_async_copy(psi, own, sems.at[0]), pltpu.make_async_copy(right, rv, sems.at[1])]
    for copy in copies:
        copy.start()
    copies[0].wait()
    last = psi.shape[0] - 1
    for out, even in zip(outs, (last, last - 1, 0, 1)):
        out[...] = own[pl.ds(jnp.where(odd == 1, last - even, even), 1)]
    copies[1].wait()


def pick(psi, right):
    vmem = pl.BlockSpec(memory_space=pltpu.VMEM)
    hbm = pl.BlockSpec(memory_space=pltpu.HBM)
    shapes = [pltpu.VMEM(psi.shape, psi.dtype), pltpu.VMEM(right.shape, right.dtype)]
    shapes += [pltpu.VMEM((1,) + psi.shape[1:], psi.dtype)] * 4
    return pl.pallas_call(
        pick_body,
        out_shape=shapes,
        in_specs=[hbm, hbm],
        out_specs=[vmem] * 6,
        scratch_shapes=[pltpu.SemaphoreType.DMA((2,))],
        compiler_params=pltpu.CompilerParams(vmem_limit_bytes=VMEM_LIMIT),
        name="pick",
    )(*(pltpu.with_memory_space_constraint(v, pltpu.HBM) for v in (psi, right)))


def entry(table, *at):
    here = True
    for axis, index in enumerate(at):
        here = here & (lax.broadcasted_iota(jnp.int32, table.shape, axis) == index)
    return jnp.sum(jnp.where(here, table.astype(jnp.float32), 0.0)).astype(jnp.int32)


def apply_body(blocks, facing, orders, couple, ops, left, rv, own, *refs):
    extras, (keep, send, mixed, inner, total) = refs[:-5], refs[-5:]
    terms, width = rv.shape[0], rv.shape[1]
    count, states = own.shape[0], own.shape[1]
    devices = len(orders[0])
    half = devices // 2
    rows = width // devices
    sec, me = lax.axis_index("sec"), lax.axis_index("term")
    base, odd = sec * count, sec % 2
    strip = 16

    for n, block in enumerate(blocks):
        s = jnp.where(odd == 1, block[1], block[0])
        for t in range(terms):
            c = entry(couple[...], t, s)
            valid = jnp.where(c >= 0, 1.0, 0.0).astype(jnp.float32)
            r = jnp.where(c >= 0, c - base, 0)
            halo = jnp.where((odd == 1) == facing, -1 - r, r - count)
            inside = (r >= 0) & (r < count)
            mine = jnp.clip(r, 0, count - 1)
            coef = [
                [
                    jnp.broadcast_to(ops[t, k : k + 1, j : j + 1] * valid, (strip, width)).astype(jnp.bfloat16)
                    for j in range(states)
                ]
                for k in range(states)
            ]
            for a in range(0, width, strip):
                source = []
                for j in range(states):
                    value = extras[0][0, j, a : a + strip, :]
                    if len(extras) > 1:
                        value = jnp.where(halo <= 0, value, extras[1][0, j, a : a + strip, :])
                    source.append(jnp.where(inside, own[mine, j, a : a + strip, :], value))
                for k in range(states):
                    value = coef[k][0] * source[0]
                    for j in range(1, states):
                        value = value + coef[k][j] * source[j]
                    mixed[t % 2, a : a + strip, k * width : (k + 1) * width] = value
            value = jnp.dot(left[t, s], mixed[t % 2], preferred_element_type=jnp.float32)
            for k in range(states):
                inner[n % 2, k * width : (k + 1) * width, t * width : (t + 1) * width] = value[
                    :, k * width : (k + 1) * width
                ].astype(jnp.bfloat16)
        total[n % 2] = jnp.dot(
            inner[n % 2], rv[...].reshape(terms * width, width), preferred_element_type=jnp.float32
        ).astype(jnp.bfloat16)
    for place in range(devices):
        slot = jnp.where(odd == 1, orders[1][place], orders[0][place])
        target = (keep, send)[place // half]
        for n in range(len(blocks)):
            for k in range(states):
                first = pl.multiple_of(k * width + (slot ^ me) * rows, rows)
                target[place % half, n, k] = total[n % 2, pl.ds(first, rows), :]


def apply_blocks(blocks, facing, orders, couple, ops, left, right, own, extras, after):
    terms, width = right.shape[0], right.shape[1]
    states = own.shape[1]
    devices = len(orders[0])
    part = pltpu.VMEM((devices // 2, len(blocks), states, width // devices, width), jnp.bfloat16)
    vmem = pl.BlockSpec(memory_space=pltpu.VMEM)
    couple, ops, left = (pltpu.with_memory_space_constraint(v, pltpu.VMEM) for v in (couple, ops, left))
    pairs = len(blocks) * terms

    def body(*refs):
        used = 5 + len(extras)
        apply_body(blocks, facing, orders, *refs[:used], *refs[used + len(after) :])

    return pl.pallas_call(
        body,
        out_shape=[part] * 2,
        in_specs=[vmem] * (5 + len(extras) + len(after)),
        out_specs=[vmem] * 2,
        scratch_shapes=[
            pltpu.VMEM((2, width, states * width), jnp.bfloat16),
            pltpu.VMEM((min(2, len(blocks)), states * width, terms * width), jnp.bfloat16),
            pltpu.VMEM((min(2, len(blocks)), states * width, width), jnp.bfloat16),
        ],
        compiler_params=pltpu.CompilerParams(vmem_limit_bytes=VMEM_LIMIT),
        cost_estimate=pl.CostEstimate(
            flops=COST * 4 * pairs * states * width**3, bytes_accessed=pairs, transcendentals=0
        ),
        name=f"apply_{blocks[0][0]}",
    )(couple, ops, left, right, own, *extras, *after)


def finish_body(groups, live, *refs):
    refs, (out, done, sems) = refs[:-3], refs[-3:]
    odd, me = lax.axis_index("sec") % 2, lax.axis_index("term")
    own, states, rows, width = out.shape
    row = lax.broadcasted_iota(jnp.int32, (rows, width), 0) + me * rows
    col = lax.broadcasted_iota(jnp.int32, (rows, width), 1)
    copies = []
    for blocks in groups:
        last = blocks is groups[-1]
        terms, refs = (refs[:3], refs[3:]) if last else (refs[:1], refs[1:])
        for n, block in enumerate(blocks):
            s = jnp.where(odd == 1, block[1], block[0])
            size = entry(live[...].reshape(1, own), 0, s)
            ok = (row < size) & (col < size)
            at = len(copies)
            for k in range(states):
                value = terms[0][0, n, k].astype(jnp.float32)
                for term in terms[1:]:
                    value = value + term[0, n, k].astype(jnp.float32)
                done[at, k] = jnp.where(ok, value, 0.0).astype(jnp.bfloat16)
            copies.append(pltpu.make_async_copy(done.at[at], out.at[s], sems.at[at]))
            copies[-1].start()
    for copy in copies:
        copy.wait()


def finish(groups, live, parts, shape):
    vmem = pl.BlockSpec(memory_space=pltpu.VMEM)
    return pl.pallas_call(
        functools.partial(finish_body, groups),
        out_shape=pltpu.HBM(shape, jnp.bfloat16),
        in_specs=[vmem] * (1 + len(parts)),
        out_specs=pl.BlockSpec(memory_space=pltpu.HBM),
        scratch_shapes=[pltpu.VMEM(shape, jnp.bfloat16), pltpu.SemaphoreType.DMA((shape[0],))],
        compiler_params=pltpu.CompilerParams(vmem_limit_bytes=VMEM_LIMIT),
        name="finish",
    )(pltpu.with_memory_space_constraint(live, pltpu.VMEM), *parts)


def on_device(psi, left, right, ops, couple, live):
    secs, devices = lax.axis_size("sec"), lax.axis_size("term")
    own, states, width = psi.shape[0], psi.shape[1], psi.shape[2]

    bits = [1 << b for b in range(devices.bit_length() - 1)]
    routes = (bits, bits[::-1])
    orders = tuple(
        tuple(sorted(range(devices), key=lambda i: [bool(i & b) for b in route])) for route in routes
    )

    chip = [(i, i ^ 1) for i in range(secs)]
    psi, right, *sends = pick(psi, right)
    beyond = [lax.ppermute(v, "sec", chip) for v in sends[:2]]
    across = [over_link(sends[2], bits[0]), over_link(sends[3], bits[-1])]
    groups = (
        (((2, 1), (3, 0)), beyond),
        (((1, 2),), across[:1]),
        (((0, 3),), across),
    )
    sums, parts, after = [], [], []
    for g, (blocks, sources) in enumerate(groups):
        keep, send = apply_blocks(blocks, g == 0, orders, couple, ops, left, right, psi, sources, after)
        after = [keep]
        got = flip(send, routes, 0)
        for step in range(1, len(bits) - 1):
            half = keep.shape[0] // 2
            total = keep + got
            keep, send = total[:half], total[half:]
            got = flip(send, routes, step)
        send = keep[1:] + got[1:]
        parts = [keep[:1], got[:1], flip(send, routes, len(bits) - 1)]
        if g < len(groups) - 1:
            sums.append(sum(v.astype(jnp.float32) for v in parts).astype(jnp.bfloat16))
    shape = (own, states, width // devices, width)
    return finish(tuple(blocks for blocks, _ in groups), live, sums + parts, shape)


def solution(mesh):
    placed = (
        P("sec", None, None, None),
        P("term", "sec", None, None),
        P("term", None, None),
        P("term", None, None),
        P("term", "sec"),
        P("sec"),
    )
    return jax.shard_map(
        on_device,
        mesh=mesh,
        in_specs=placed,
        out_specs=P("sec", None, "term", None),
        check_vma=False,
    )
```

time: 150 us -> 34.2 us (0.23)
  the two profiles are of different devices: /device:TPU:0 before, /device:TPU:22 now
where the time goes in v2:
time: 34.2 us; the launch traced here: 34 us
  waiting for transfers between devices  17 us (50%)
  Pallas kernels  10.4 us (30%)
  starting transfers between devices  6.3 us (18%)
    ppermute x6, waiting for transfers between devices, flip(): return lax.ppermute(value, ('sec', 'term'), pairs)  11.2 us
    pallas_call x3, Pallas kernels, apply_blocks(): pl.pallas_call(body, out_shape=[part] * 2, in_specs=[vmem] * (5 + len(ext...  7.53 us
    ppermute x2, waiting for transfers between devices, over_link(): return lax.ppermute(value, ('sec', 'term'), pairs)  5.36 us
    ppermute x6, starting transfers between devices, flip(): return lax.ppermute(value, ('sec', 'term'), pairs)  3.99 us
    pallas_call x1, Pallas kernels, pick(): pl.pallas_call(pick_body, out_shape=shapes, in_specs=[hbm, hbm], out_spec...  1.9 us
    ppermute x2, starting transfers between devices, over_link(): return lax.ppermute(value, ('sec', 'term'), pairs)  1.75 us
    pallas_call x1, Pallas kernels, finish(): pl.pallas_call(functools.partial(finish_body, groups), out_shape=pltpu.HB...  0.97 us
  transfers between devices with their start and end apart: 10, of which 7 were waited for; matrix products, arithmetic and copies ran while one was open for 1% of the time, Pallas kernels for 22%

profile of v2, /device:TPU:22, one launch (start us, length us, event | category | flops | bytes accessed | tf_op | source)
XLA Modules:
  0.0 34.0 jit_solution(1285982453468378892)
XLA Ops:
  0.0 1.9 %pick.1 = (bf16[4,4,256,256]{3,2,1,0:T(8,128)(2,1)S(1)}, bf16[4,256,256]{2,1,0:T(8,128)(2,1)S(1)}, bf16[1,4,256,256]{3,2,1,0:T(8,128)(2,1)S(1)}, bf16[1,4,256,25...) custom-call(bf16[4,4,256,256]{3,2,1,0:T(8,128)(2,1)} %psi.1, ...), custom_call_target="tpu_custom_call" | custom-call | tf_op jit(solution)/shard_map/pick/pallas_call | solution.py:52
  1.9 0.1 collective-permute-start
  2.0 0.5 %collective-permute-start.1 = (bf16[1,4,256,256]{3,2,1,0:T(8,128)(2,1)S(1)}, bf16[1,4,256,256]{3,2,1,0:T(8,128)(2,1)S(1)}, u32[]{:S(2)}, u32[]{:S(2)}) collective-permute-start(bf16[1,4,256,256]{3,2,1,0:T(8,128)(2,1)S(1)} %get-tuple-element.20), channel_id=1, source_target_pairs={{0,4},{4,0},{8,12},{12,8},{16,20},{20,16},{24,28},{28,24},{1,5},{5... | collective-permute-start | bytes 1572872 | tf_op jit(solution)/shard_map/ppermute | solution.py:208
  2.5 0.1 collective-permute-start.4
  2.6 1.6 %collective-permute-start.7 = (bf16[1,4,256,256]{3,2,1,0:T(8,128)(2,1)S(1)}, bf16[1,4,256,256]{3,2,1,0:T(8,128)(2,1)S(1)}, u32[]{:S(2)}, u32[]{:S(2)}) collective-permute-start(bf16[1,4,256,256]{3,2,1,0:T(8,128)(2,1)S(1)} %get-tuple-element.26), channel_id=1, source_target_pairs={{0,2},{1,3},{2,0},{3,1},{4,8},{5,9},{6,10},{7,11},{8,4},{9,5},{10,... | collective-permute-start | bytes 1572872 | tf_op jit(solution)/shard_map/ppermute | solution.py:31
  4.2 0.4 %collective-permute-done.1.refs_6_ = bf16[1,4,256,256]{3,2,1,0:T(8,128)(2,1)S(1)} collective-permute-done((bf16[1,4,256,256]{3,2,1,0:T(8,128)(2,1)S(1)}, bf16[1,4,256,256]{3,2,1,0:T(8,128)(2,1)S(1)}, u32[]{:S(2)}, u32[]{:S(2)}) %collective-permute-start.1) | collective-permute-done | bytes 524320 | tf_op jit(solution)/shard_map/ppermute | solution.py:208
  4.7 3.6 %apply_2.1 = (bf16[2,2,4,64,256]{4,3,2,1,0:T(8,128)(2,1)S(1)}, bf16[2,2,4,64,256]{4,3,2,1,0:T(8,128)(2,1)S(1)}) custom-call(s32[4,4]{1,0:T(4,128)S(1)} %copy-done.3, f32[4,4,4]{2,1,0:T(4,128)S(1)} %copy-done.2, bf16[4,4,256,256]{3,2,1,0:T(8,128)(2,1)S(1)} %copy-done.1, bf16[4,256,256]{2,1,0:T(8,128)(2,1)S(1)} %get-tuple-element.17.refs_3_, ...), custom_call_target="tpu_custom_call" | custom-call | flops 21474836480 | bytes 8 | tf_op jit(solution)/shard_map/apply_2/pallas_call | solution.py:139
  8.2 0.6 %collective-permute-start.2 = (bf16[2,2,4,64,256]{4,3,2,1,0:T(8,128)(2,1)S(1)}, bf16[2,2,4,64,256]{4,3,2,1,0:T(8,128)(2,1)S(1)}, u32[]{:S(2)}, u32[]{:S(2)}) collective-permute-start(bf16[2,2,4,64,256]{4,3,2,1,0:T(8,128)(2,1)S(1)} %get-tuple-element.22), channel_id=1, source_target_pairs={{0,1},{1,0},{2,3},{3,2},{4,6},{5,7},{6,4},{7,5},{8,9},{9,8},{10,11... | collective-permute-start | bytes 1572872 | tf_op jit(solution)/shard_map/ppermute | solution.py:20
  8.8 2.3 %collective-permute-done.4.refs_5_ = bf16[1,4,256,256]{3,2,1,0:T(8,128)(2,1)S(1)} collective-permute-done((bf16[1,4,256,256]{3,2,1,0:T(8,128)(2,1)S(1)}, bf16[1,4,256,256]{3,2,1,0:T(8,128)(2,1)S(1)}, u32[]{:S(2)}, u32[]{:S(2)}) %collective-permute-start.4) | collective-permute-done | bytes 524320 | tf_op jit(solution)/shard_map/ppermute | solution.py:31
  11.1 1.9 %apply_1.1 = (bf16[2,1,4,64,256]{4,3,2,1,0:T(8,128)(2,1)S(1)}, bf16[2,1,4,64,256]{4,3,2,1,0:T(8,128)(2,1)S(1)}) custom-call(s32[4,4]{1,0:T(4,128)S(1)} %copy-done.3, f32[4,4,4]{2,1,0:T(4,128)S(1)} %copy-done.2, bf16[4,4,256,256]{3,2,1,0:T(8,128)(2,1)S(1)} %copy-done.1, bf16[4,256,256]{2,1,0:T(8,128)(2,1)S(1)} %get-tuple-element.17.refs_3_, ...), custom_call_target="tpu_custom_call" | custom-call | flops 10737418240 | bytes 4 | tf_op jit(solution)/shard_map/apply_1/pallas_call | solution.py:139
  13.0 0.6 %collective-permute-start.5 = (bf16[2,1,4,64,256]{4,3,2,1,0:T(8,128)(2,1)S(1)}, bf16[2,1,4,64,256]{4,3,2,1,0:T(8,128)(2,1)S(1)}, u32[]{:S(2)}, u32[]{:S(2)}) collective-permute-start(bf16[2,1,4,64,256]{4,3,2,1,0:T(8,128)(2,1)S(1)} %get-tuple-element.25), channel_id=1, source_target_pairs={{0,1},{1,0},{2,3},{3,2},{4,6},{5,7},{6,4},{7,5},{8,9},{9,8},{10,11... | collective-permute-start | bytes 786440 | tf_op jit(solution)/shard_map/ppermute | solution.py:20
  13.6 3.1 %collective-permute-done.7.refs_6_ = bf16[1,4,256,256]{3,2,1,0:T(8,128)(2,1)S(1)} collective-permute-done((bf16[1,4,256,256]{3,2,1,0:T(8,128)(2,1)S(1)}, bf16[1,4,256,256]{3,2,1,0:T(8,128)(2,1)S(1)}, u32[]{:S(2)}, u32[]{:S(2)}) %collective-permute-start.7) | collective-permute-done | bytes 524320 | tf_op jit(solution)/shard_map/ppermute | solution.py:31
  16.7 2.0 %apply_0.1 = (bf16[2,1,4,64,256]{4,3,2,1,0:T(8,128)(2,1)S(1)}, bf16[2,1,4,64,256]{4,3,2,1,0:T(8,128)(2,1)S(1)}) custom-call(s32[4,4]{1,0:T(4,128)S(1)} %copy-done.3, f32[4,4,4]{2,1,0:T(4,128)S(1)} %copy-done.2, bf16[4,4,256,256]{3,2,1,0:T(8,128)(2,1)S(1)} %copy-done.1, bf16[4,256,256]{2,1,0:T(8,128)(2,1)S(1)} %get-tuple-element.17.refs_3_, ...), custom_call_target="tpu_custom_call" | custom-call | flops 10737418240 | bytes 4 | tf_op jit(solution)/shard_map/apply_0/pallas_call | solution.py:139
  18.7 0.6 %collective-permute-start.8 = (bf16[2,1,4,64,256]{4,3,2,1,0:T(8,128)(2,1)S(1)}, bf16[2,1,4,64,256]{4,3,2,1,0:T(8,128)(2,1)S(1)}, u32[]{:S(2)}, u32[]{:S(2)}) collective-permute-start(bf16[2,1,4,64,256]{4,3,2,1,0:T(8,128)(2,1)S(1)} %get-tuple-element.28), channel_id=1, source_target_pairs={{0,1},{1,0},{2,3},{3,2},{4,6},{5,7},{6,4},{7,5},{8,9},{9,8},{10,11... | collective-permute-start | bytes 786440 | tf_op jit(solution)/shard_map/ppermute | solution.py:20
  19.3 1.0 %collective-permute-done.5 = bf16[2,1,4,64,256]{4,3,2,1,0:T(8,128)(2,1)S(1)} collective-permute-done((bf16[2,1,4,64,256]{4,3,2,1,0:T(8,128)(2,1)S(1)}, bf16[2,1,4,64,256]{4,3,2,1,0:T(8,128)(2,1)S(1)}, u32[]{:S(2)}, u32[]{:S(2)}) %collective-permute-start.5) | collective-permute-done | bytes 262176 | tf_op jit(solution)/shard_map/ppermute | solution.py:20
  20.3 0.6 %collective-permute-start.6 = (bf16[1,1,4,64,256]{4,3,2,1,0:T(8,128)(2,1)S(1)}, bf16[1,1,4,64,256]{4,3,2,1,0:T(8,128)(2,1)S(1)}, u32[]{:S(2)}, u32[]{:S(2)}) collective-permute-start(bf16[1,1,4,64,256]{4,3,2,1,0:T(8,128)(2,1)S(1)} %slice_add_fusion.2), channel_id=1, source_target_pairs={{0,2},{1,3},{2,0},{3,1},{4,5},{5,4},{6,7},{7,6},{8,10},{9,11},{10,... | collective-permute-start | bytes 393224 | tf_op jit(solution)/shard_map/ppermute | solution.py:20
  20.9 1.6 %collective-permute-start.3 = (bf16[1,2,4,64,256]{4,3,2,1,0:T(8,128)(2,1)S(1)}, bf16[1,2,4,64,256]{4,3,2,1,0:T(8,128)(2,1)S(1)}, u32[]{:S(2)}, u32[]{:S(2)}) collective-permute-start(bf16[1,2,4,64,256]{4,3,2,1,0:T(8,128)(2,1)S(1)} %slice_add_fusion), channel_id=1, source_target_pairs={{0,2},{1,3},{2,0},{3,1},{4,5},{5,4},{6,7},{7,6},{8,10},{9,11},{10,... | collective-permute-start | bytes 786440 | tf_op jit(solution)/shard_map/ppermute | solution.py:20
  22.5 5.5 %collective-permute-done.8 = bf16[2,1,4,64,256]{4,3,2,1,0:T(8,128)(2,1)S(1)} collective-permute-done((bf16[2,1,4,64,256]{4,3,2,1,0:T(8,128)(2,1)S(1)}, bf16[2,1,4,64,256]{4,3,2,1,0:T(8,128)(2,1)S(1)}, u32[]{:S(2)}, u32[]{:S(2)}) %collective-permute-start.8) | collective-permute-done | bytes 262176 | tf_op jit(solution)/shard_map/ppermute | solution.py:20
  28.0 0.1 collective-permute-start.9
  28.1 0.1 add_convert_fusion.1.refs_1_
  28.2 0.6 %collective-permute-done.3 = bf16[1,2,4,64,256]{4,3,2,1,0:T(8,128)(2,1)S(1)} collective-permute-done((bf16[1,2,4,64,256]{4,3,2,1,0:T(8,128)(2,1)S(1)}, bf16[1,2,4,64,256]{4,3,2,1,0:T(8,128)(2,1)S(1)}, u32[]{:S(2)}, u32[]{:S(2)}) %collective-permute-start.3) | collective-permute-done | bytes 262176 | tf_op jit(solution)/shard_map/ppermute | solution.py:20
  28.8 0.1 add_convert_fusion.refs_0_
  28.9 4.1 %collective-permute-done.9.refs_4_ = bf16[1,1,4,64,256]{4,3,2,1,0:T(8,128)(2,1)S(1)} collective-permute-done((bf16[1,1,4,64,256]{4,3,2,1,0:T(8,128)(2,1)S(1)}, bf16[1,1,4,64,256]{4,3,2,1,0:T(8,128)(2,1)S(1)}, u32[]{:S(2)}, u32[]{:S(2)}) %collective-permute-start.9) | collective-permute-done | bytes 131104 | tf_op jit(solution)/shard_map/ppermute | solution.py:20
  33.1 1.0 %finish.1 = bf16[4,4,64,256]{3,2,1,0:T(8,128)(2,1)} custom-call(s32[4]{0:T(128)S(1)} %copy-done, bf16[1,2,4,64,256]{4,3,2,1,0:T(8,128)(2,1)S(1)} %add_convert_fusion.refs_0_, bf16[1,1,4,64,256]{4,3,2,1,0:T(8,128)(2,1)S(1)} %add_convert_fusion.1.refs_1_, bf16[1,1,4,64,256]{4,3,2,1,0:T(8,128)(2,1)S(1)} %get-tuple-element.30.refs_2_, ...), custom_call_target="tpu_custom_call" | custom-call | tf_op jit(solution)/shard_map/finish/pallas_call | solution.py:185
  (14 shorter events, 0.1 us)
Async XLA Ops:
  0.0 4.6 %copy-start.3 = (s32[4,4]{1,0:T(4,128)S(1)}, s32[4,4]{1,0:T(4,128)}, u32[]{:S(2)}) copy-start(s32[4,4]{1,0:T(4,128)} %refs_0_.5) | copy-start | bytes 196
  0.0 4.6 %copy-start.2 = (f32[4,4,4]{2,1,0:T(4,128)S(1)}, f32[4,4,4]{2,1,0:T(4,128)}, u32[]{:S(2)}) copy-start(f32[4,4,4]{2,1,0:T(4,128)} %refs_1_.5) | copy-start | bytes 772
  0.0 4.6 %copy-start.1 = (bf16[4,4,256,256]{3,2,1,0:T(8,128)(2,1)S(1)}, bf16[4,4,256,256]{3,2,1,0:T(8,128)(2,1)}, u32[]{:S(2)}) copy-start(bf16[4,4,256,256]{3,2,1,0:T(8,128)(2,1)} %refs_2_.5) | copy-start | bytes 6291460
  1.9 2.3 %collective-permute-start = (bf16[1,4,256,256]{3,2,1,0:T(8,128)(2,1)S(1)}, bf16[1,4,256,256]{3,2,1,0:T(8,128)(2,1)S(1)}, u32[]{:S(2)}, u32[]{:S(2)}) collective-permute-start(bf16[1,4,256,256]{3,2,1,0:T(8,128)(2,1)S(1)} %get-tuple-element.19), channel_id=1, source_target_pairs={{0,4},{4,0},{8,12},{12,8},{16,20},{20,16},{24,28},{28,24},{1,5},{5... | collective-permute-start | bytes 1572872 | tf_op jit(solution)/shard_map/ppermute | solution.py:208
  2.0 2.6 %collective-permute-start.1 = (bf16[1,4,256,256]{3,2,1,0:T(8,128)(2,1)S(1)}, bf16[1,4,256,256]{3,2,1,0:T(8,128)(2,1)S(1)}, u32[]{:S(2)}, u32[]{:S(2)}) collective-permute-start(bf16[1,4,256,256]{3,2,1,0:T(8,128)(2,1)S(1)} %get-tuple-element.20), channel_id=1, source_target_pairs={{0,4},{4,0},{8,12},{12,8},{16,20},{20,16},{24,28},{28,24},{1,5},{5... | collective-permute-start | bytes 1572872 | tf_op jit(solution)/shard_map/ppermute | solution.py:208
  2.5 8.6 %collective-permute-start.4 = (bf16[1,4,256,256]{3,2,1,0:T(8,128)(2,1)S(1)}, bf16[1,4,256,256]{3,2,1,0:T(8,128)(2,1)S(1)}, u32[]{:S(2)}, u32[]{:S(2)}) collective-permute-start(bf16[1,4,256,256]{3,2,1,0:T(8,128)(2,1)S(1)} %get-tuple-element.23), channel_id=1, source_target_pairs={{0,1},{1,0},{2,3},{3,2},{4,8},{5,9},{6,10},{7,11},{8,4},{9,5},{10,... | collective-permute-start | bytes 1572872 | tf_op jit(solution)/shard_map/ppermute | solution.py:31
  2.6 14.1 %collective-permute-start.7 = (bf16[1,4,256,256]{3,2,1,0:T(8,128)(2,1)S(1)}, bf16[1,4,256,256]{3,2,1,0:T(8,128)(2,1)S(1)}, u32[]{:S(2)}, u32[]{:S(2)}) collective-permute-start(bf16[1,4,256,256]{3,2,1,0:T(8,128)(2,1)S(1)} %get-tuple-element.26), channel_id=1, source_target_pairs={{0,2},{1,3},{2,0},{3,1},{4,8},{5,9},{6,10},{7,11},{8,4},{9,5},{10,... | collective-permute-start | bytes 1572872 | tf_op jit(solution)/shard_map/ppermute | solution.py:31
  8.2 12.6 %collective-permute-start.2 = (bf16[2,2,4,64,256]{4,3,2,1,0:T(8,128)(2,1)S(1)}, bf16[2,2,4,64,256]{4,3,2,1,0:T(8,128)(2,1)S(1)}, u32[]{:S(2)}, u32[]{:S(2)}) collective-permute-start(bf16[2,2,4,64,256]{4,3,2,1,0:T(8,128)(2,1)S(1)} %get-tuple-element.22), channel_id=1, source_target_pairs={{0,1},{1,0},{2,3},{3,2},{4,6},{5,7},{6,4},{7,5},{8,9},{9,8},{10,11... | collective-permute-start | bytes 1572872 | tf_op jit(solution)/shard_map/ppermute | solution.py:20
  13.0 7.3 %collective-permute-start.5 = (bf16[2,1,4,64,256]{4,3,2,1,0:T(8,128)(2,1)S(1)}, bf16[2,1,4,64,256]{4,3,2,1,0:T(8,128)(2,1)S(1)}, u32[]{:S(2)}, u32[]{:S(2)}) collective-permute-start(bf16[2,1,4,64,256]{4,3,2,1,0:T(8,128)(2,1)S(1)} %get-tuple-element.25), channel_id=1, source_target_pairs={{0,1},{1,0},{2,3},{3,2},{4,6},{5,7},{6,4},{7,5},{8,9},{9,8},{10,11... | collective-permute-start | bytes 786440 | tf_op jit(solution)/shard_map/ppermute | solution.py:20
  18.7 14.3 %copy-start = (s32[4]{0:T(128)S(1)}, s32[4]{0:T(128)}, u32[]{:S(2)}) copy-start(s32[4]{0:T(128)} %live.1) | copy-start | bytes 52
  18.7 9.2 %collective-permute-start.8 = (bf16[2,1,4,64,256]{4,3,2,1,0:T(8,128)(2,1)S(1)}, bf16[2,1,4,64,256]{4,3,2,1,0:T(8,128)(2,1)S(1)}, u32[]{:S(2)}, u32[]{:S(2)}) collective-permute-start(bf16[2,1,4,64,256]{4,3,2,1,0:T(8,128)(2,1)S(1)} %get-tuple-element.28), channel_id=1, source_target_pairs={{0,1},{1,0},{2,3},{3,2},{4,6},{5,7},{6,4},{7,5},{8,9},{9,8},{10,11... | collective-permute-start | bytes 786440 | tf_op jit(solution)/shard_map/ppermute | solution.py:20
  20.3 7.8 %collective-permute-start.6 = (bf16[1,1,4,64,256]{4,3,2,1,0:T(8,128)(2,1)S(1)}, bf16[1,1,4,64,256]{4,3,2,1,0:T(8,128)(2,1)S(1)}, u32[]{:S(2)}, u32[]{:S(2)}) collective-permute-start(bf16[1,1,4,64,256]{4,3,2,1,0:T(8,128)(2,1)S(1)} %slice_add_fusion.2), channel_id=1, source_target_pairs={{0,2},{1,3},{2,0},{3,1},{4,5},{5,4},{6,7},{7,6},{8,10},{9,11},{10,... | collective-permute-start | bytes 393224 | tf_op jit(solution)/shard_map/ppermute | solution.py:20
  20.9 7.9 %collective-permute-start.3 = (bf16[1,2,4,64,256]{4,3,2,1,0:T(8,128)(2,1)S(1)}, bf16[1,2,4,64,256]{4,3,2,1,0:T(8,128)(2,1)S(1)}, u32[]{:S(2)}, u32[]{:S(2)}) collective-permute-start(bf16[1,2,4,64,256]{4,3,2,1,0:T(8,128)(2,1)S(1)} %slice_add_fusion), channel_id=1, source_target_pairs={{0,2},{1,3},{2,0},{3,1},{4,5},{5,4},{6,7},{7,6},{8,10},{9,11},{10,... | collective-permute-start | bytes 786440 | tf_op jit(solution)/shard_map/ppermute | solution.py:20
  28.0 5.0 %collective-permute-start.9 = (bf16[1,1,4,64,256]{4,3,2,1,0:T(8,128)(2,1)S(1)}, bf16[1,1,4,64,256]{4,3,2,1,0:T(8,128)(2,1)S(1)}, u32[]{:S(2)}, u32[]{:S(2)}) collective-permute-start(bf16[1,1,4,64,256]{4,3,2,1,0:T(8,128)(2,1)S(1)} %get-tuple-element.29), channel_id=1, source_target_pairs={{0,2},{1,3},{2,0},{3,1},{4,5},{5,4},{6,7},{7,6},{8,10},{9,11},{10,... | collective-permute-start | bytes 393224 | tf_op jit(solution)/shard_map/ppermute | solution.py:20

commit v3 on v2

--- a/solution.py
+++ b/solution.py
@@ -9,6 +9,7 @@
 
 VMEM_LIMIT = 24 * 1024 * 1024
 COST = 10
+WAYS = (0, 0, 1)
 
 
 def flip(value, routes, step):
@@ -198,10 +199,7 @@
     own, states, width = psi.shape[0], psi.shape[1], psi.shape[2]
 
     bits = [1 << b for b in range(devices.bit_length() - 1)]
-    routes = (bits, bits[::-1])
-    orders = tuple(
-        tuple(sorted(range(devices), key=lambda i: [bool(i & b) for b in route])) for route in routes
-    )
+    ways = ((bits, bits[::-1]), (bits[::-1], bits))
 
     chip = [(i, i ^ 1) for i in range(secs)]
     psi, right, *sends = pick(psi, right)
@@ -214,6 +212,10 @@
     )
     sums, parts, after = [], [], []
     for g, (blocks, sources) in enumerate(groups):
+        routes = ways[WAYS[g]]
+        orders = tuple(
+            tuple(sorted(range(devices), key=lambda i: [bool(i & b) for b in route])) for route in routes
+        )
         keep, send = apply_blocks(blocks, g == 0, orders, couple, ops, left, right, psi, sources, after)
         after = [keep]
         got = flip(send, routes, 0)

time: 34.2 us -> 33.1 us (0.968)
  the two profiles are of different devices: /device:TPU:22 before, /device:TPU:0 now
where the time goes in v3:
time: 33.1 us; the launch traced here: 33 us
  starting transfers between devices  11.4 us (34%)
  waiting for transfers between devices  10.8 us (33%)
  Pallas kernels  10.4 us (31%)
    ppermute x6, waiting for transfers between devices, flip(): return lax.ppermute(value, ('sec', 'term'), pairs)  9.18 us
    pallas_call x3, Pallas kernels, apply_blocks(): pl.pallas_call(body, out_shape=[part] * 2, in_specs=[vmem] * (5 + len(ext...  7.49 us
    ppermute x6, starting transfers between devices, flip(): return lax.ppermute(value, ('sec', 'term'), pairs)  6.37 us
    ppermute x2, starting transfers between devices, over_link(): return lax.ppermute(value, ('sec', 'term'), pairs)  4.44 us
    pallas_call x1, Pallas kernels, pick(): pl.pallas_call(pick_body, out_shape=shapes, in_specs=[hbm, hbm], out_spec...  1.89 us
    ppermute x2, waiting for transfers between devices, over_link(): return lax.ppermute(value, ('sec', 'term'), pairs)  1.66 us
    pallas_call x1, Pallas kernels, finish(): pl.pallas_call(functools.partial(finish_body, groups), out_shape=pltpu.HB...  0.98 us
  transfers between devices with their start and end apart: 10, of which 6 were waited for; matrix products, arithmetic and copies ran while one was open for 1% of the time, Pallas kernels for 23%

profile of v3, /device:TPU:0, one launch (start us, length us, event | category | flops | bytes accessed | tf_op | source)
XLA Modules:
  0.0 33.0 jit_solution(17154721434364432375)
XLA Ops:
  0.0 1.9 %pick.1 = (bf16[4,4,256,256]{3,2,1,0:T(8,128)(2,1)S(1)}, bf16[4,256,256]{2,1,0:T(8,128)(2,1)S(1)}, bf16[1,4,256,256]{3,2,1,0:T(8,128)(2,1)S(1)}, bf16[1,4,256,25...) custom-call(bf16[4,4,256,256]{3,2,1,0:T(8,128)(2,1)} %psi.1, ...), custom_call_target="tpu_custom_call" | custom-call | tf_op jit(solution)/shard_map/pick/pallas_call | solution.py:53
  1.9 0.5 %collective-permute-start = (bf16[1,4,256,256]{3,2,1,0:T(8,128)(2,1)S(1)}, bf16[1,4,256,256]{3,2,1,0:T(8,128)(2,1)S(1)}, u32[]{:S(2)}, u32[]{:S(2)}) collective-permute-start(bf16[1,4,256,256]{3,2,1,0:T(8,128)(2,1)S(1)} %get-tuple-element.19), channel_id=1, source_target_pairs={{0,4},{4,0},{8,12},{12,8},{16,20},{20,16},{24,28},{28,24},{1,5},{5... | collective-permute-start | bytes 1572872 | tf_op jit(solution)/shard_map/ppermute | solution.py:206
  2.4 0.1 collective-permute-start.1
  2.5 2.9 %collective-permute-start.4 = (bf16[1,4,256,256]{3,2,1,0:T(8,128)(2,1)S(1)}, bf16[1,4,256,256]{3,2,1,0:T(8,128)(2,1)S(1)}, u32[]{:S(2)}, u32[]{:S(2)}) collective-permute-start(bf16[1,4,256,256]{3,2,1,0:T(8,128)(2,1)S(1)} %get-tuple-element.23), channel_id=1, source_target_pairs={{0,1},{1,0},{2,3},{3,2},{4,8},{5,9},{6,10},{7,11},{8,4},{9,5},{10,... | collective-permute-start | bytes 1572872 | tf_op jit(solution)/shard_map/ppermute | solution.py:32
  5.4 1.5 %collective-permute-start.7 = (bf16[1,4,256,256]{3,2,1,0:T(8,128)(2,1)S(1)}, bf16[1,4,256,256]{3,2,1,0:T(8,128)(2,1)S(1)}, u32[]{:S(2)}, u32[]{:S(2)}) collective-permute-start(bf16[1,4,256,256]{3,2,1,0:T(8,128)(2,1)S(1)} %get-tuple-element.26), channel_id=1, source_target_pairs={{0,2},{1,3},{2,0},{3,1},{4,8},{5,9},{6,10},{7,11},{8,4},{9,5},{10,... | collective-permute-start | bytes 1572872 | tf_op jit(solution)/shard_map/ppermute | solution.py:32
  7.0 3.6 %apply_2.1 = (bf16[2,2,4,64,256]{4,3,2,1,0:T(8,128)(2,1)S(1)}, bf16[2,2,4,64,256]{4,3,2,1,0:T(8,128)(2,1)S(1)}) custom-call(s32[4,4]{1,0:T(4,128)S(1)} %copy-done.3, f32[4,4,4]{2,1,0:T(4,128)S(1)} %copy-done.2, bf16[4,4,256,256]{3,2,1,0:T(8,128)(2,1)S(1)} %copy-done.1, bf16[4,256,256]{2,1,0:T(8,128)(2,1)S(1)} %get-tuple-element.17.refs_3_, ...), custom_call_target="tpu_custom_call" | custom-call | flops 21474836480 | bytes 8 | tf_op jit(solution)/shard_map/apply_2/pallas_call | solution.py:140
  10.6 0.7 %collective-permute-start.2 = (bf16[2,2,4,64,256]{4,3,2,1,0:T(8,128)(2,1)S(1)}, bf16[2,2,4,64,256]{4,3,2,1,0:T(8,128)(2,1)S(1)}, u32[]{:S(2)}, u32[]{:S(2)}) collective-permute-start(bf16[2,2,4,64,256]{4,3,2,1,0:T(8,128)(2,1)S(1)} %get-tuple-element.22), channel_id=1, source_target_pairs={{0,1},{1,0},{2,3},{3,2},{4,6},{5,7},{6,4},{7,5},{8,9},{9,8},{10,11... | collective-permute-start | bytes 1572872 | tf_op jit(solution)/shard_map/ppermute | solution.py:21
  11.2 1.4 %collective-permute-done.4.refs_5_ = bf16[1,4,256,256]{3,2,1,0:T(8,128)(2,1)S(1)} collective-permute-done((bf16[1,4,256,256]{3,2,1,0:T(8,128)(2,1)S(1)}, bf16[1,4,256,256]{3,2,1,0:T(8,128)(2,1)S(1)}, u32[]{:S(2)}, u32[]{:S(2)}) %collective-permute-start.4) | collective-permute-done | bytes 524320 | tf_op jit(solution)/shard_map/ppermute | solution.py:32
  12.6 1.9 %apply_1.1 = (bf16[2,1,4,64,256]{4,3,2,1,0:T(8,128)(2,1)S(1)}, bf16[2,1,4,64,256]{4,3,2,1,0:T(8,128)(2,1)S(1)}) custom-call(s32[4,4]{1,0:T(4,128)S(1)} %copy-done.3, f32[4,4,4]{2,1,0:T(4,128)S(1)} %copy-done.2, bf16[4,4,256,256]{3,2,1,0:T(8,128)(2,1)S(1)} %copy-done.1, bf16[4,256,256]{2,1,0:T(8,128)(2,1)S(1)} %get-tuple-element.17.refs_3_, ...), custom_call_target="tpu_custom_call" | custom-call | flops 10737418240 | bytes 4 | tf_op jit(solution)/shard_map/apply_1/pallas_call | solution.py:140
  14.5 2.1 %collective-permute-start.5 = (bf16[2,1,4,64,256]{4,3,2,1,0:T(8,128)(2,1)S(1)}, bf16[2,1,4,64,256]{4,3,2,1,0:T(8,128)(2,1)S(1)}, u32[]{:S(2)}, u32[]{:S(2)}) collective-permute-start(bf16[2,1,4,64,256]{4,3,2,1,0:T(8,128)(2,1)S(1)} %get-tuple-element.25), channel_id=1, source_target_pairs={{0,1},{1,0},{2,3},{3,2},{4,6},{5,7},{6,4},{7,5},{8,9},{9,8},{10,11... | collective-permute-start | bytes 786440 | tf_op jit(solution)/shard_map/ppermute | solution.py:21
  16.6 0.3 collective-permute-done.7.refs_6_
  16.9 2.0 %apply_0.1 = (bf16[2,1,4,64,256]{4,3,2,1,0:T(8,128)(2,1)S(1)}, bf16[2,1,4,64,256]{4,3,2,1,0:T(8,128)(2,1)S(1)}) custom-call(s32[4,4]{1,0:T(4,128)S(1)} %copy-done.3, f32[4,4,4]{2,1,0:T(4,128)S(1)} %copy-done.2, bf16[4,4,256,256]{3,2,1,0:T(8,128)(2,1)S(1)} %copy-done.1, bf16[4,256,256]{2,1,0:T(8,128)(2,1)S(1)} %get-tuple-element.17.refs_3_, ...), custom_call_target="tpu_custom_call" | custom-call | flops 10737418240 | bytes 4 | tf_op jit(solution)/shard_map/apply_0/pallas_call | solution.py:140
  18.9 0.0 copy-start
  18.9 1.4 %collective-permute-start.8 = (bf16[2,1,4,64,256]{4,3,2,1,0:T(8,128)(2,1)S(1)}, bf16[2,1,4,64,256]{4,3,2,1,0:T(8,128)(2,1)S(1)}, u32[]{:S(2)}, u32[]{:S(2)}) collective-permute-start(bf16[2,1,4,64,256]{4,3,2,1,0:T(8,128)(2,1)S(1)} %get-tuple-element.28), channel_id=1, source_target_pairs={{0,2},{1,3},{2,0},{3,1},{4,5},{5,4},{6,7},{7,6},{8,10},{9,11},{10,... | collective-permute-start | bytes 786440 | tf_op jit(solution)/shard_map/ppermute | solution.py:21
  20.3 2.3 %collective-permute-done.5 = bf16[2,1,4,64,256]{4,3,2,1,0:T(8,128)(2,1)S(1)} collective-permute-done((bf16[2,1,4,64,256]{4,3,2,1,0:T(8,128)(2,1)S(1)}, bf16[2,1,4,64,256]{4,3,2,1,0:T(8,128)(2,1)S(1)}, u32[]{:S(2)}, u32[]{:S(2)}) %collective-permute-start.5) | collective-permute-done | bytes 262176 | tf_op jit(solution)/shard_map/ppermute | solution.py:21
  22.6 0.7 %collective-permute-start.6 = (bf16[1,1,4,64,256]{4,3,2,1,0:T(8,128)(2,1)S(1)}, bf16[1,1,4,64,256]{4,3,2,1,0:T(8,128)(2,1)S(1)}, u32[]{:S(2)}, u32[]{:S(2)}) collective-permute-start(bf16[1,1,4,64,256]{4,3,2,1,0:T(8,128)(2,1)S(1)} %slice_add_fusion.2), channel_id=1, source_target_pairs={{0,2},{1,3},{2,0},{3,1},{4,5},{5,4},{6,7},{7,6},{8,10},{9,11},{10,... | collective-permute-start | bytes 393224 | tf_op jit(solution)/shard_map/ppermute | solution.py:21
  23.4 1.5 %collective-permute-start.3 = (bf16[1,2,4,64,256]{4,3,2,1,0:T(8,128)(2,1)S(1)}, bf16[1,2,4,64,256]{4,3,2,1,0:T(8,128)(2,1)S(1)}, u32[]{:S(2)}, u32[]{:S(2)}) collective-permute-start(bf16[1,2,4,64,256]{4,3,2,1,0:T(8,128)(2,1)S(1)} %slice_add_fusion), channel_id=1, source_target_pairs={{0,2},{1,3},{2,0},{3,1},{4,5},{5,4},{6,7},{7,6},{8,10},{9,11},{10,... | collective-permute-start | bytes 786440 | tf_op jit(solution)/shard_map/ppermute | solution.py:21
  24.8 1.0 %collective-permute-done.8 = bf16[2,1,4,64,256]{4,3,2,1,0:T(8,128)(2,1)S(1)} collective-permute-done((bf16[2,1,4,64,256]{4,3,2,1,0:T(8,128)(2,1)S(1)}, bf16[2,1,4,64,256]{4,3,2,1,0:T(8,128)(2,1)S(1)}, u32[]{:S(2)}, u32[]{:S(2)}) %collective-permute-start.8) | collective-permute-done | bytes 262176 | tf_op jit(solution)/shard_map/ppermute | solution.py:21
  25.9 0.1 collective-permute-start.9
  26.0 1.7 %collective-permute-done.6 = bf16[1,1,4,64,256]{4,3,2,1,0:T(8,128)(2,1)S(1)} collective-permute-done((bf16[1,1,4,64,256]{4,3,2,1,0:T(8,128)(2,1)S(1)}, bf16[1,1,4,64,256]{4,3,2,1,0:T(8,128)(2,1)S(1)}, u32[]{:S(2)}, u32[]{:S(2)}) %collective-permute-start.6) | collective-permute-done | bytes 131104 | tf_op jit(solution)/shard_map/ppermute | solution.py:21
  27.7 0.1 add_convert_fusion.1.refs_1_
  27.7 4.2 %collective-permute-done.3 = bf16[1,2,4,64,256]{4,3,2,1,0:T(8,128)(2,1)S(1)} collective-permute-done((bf16[1,2,4,64,256]{4,3,2,1,0:T(8,128)(2,1)S(1)}, bf16[1,2,4,64,256]{4,3,2,1,0:T(8,128)(2,1)S(1)}, u32[]{:S(2)}, u32[]{:S(2)}) %collective-permute-start.3) | collective-permute-done | bytes 262176 | tf_op jit(solution)/shard_map/ppermute | solution.py:21
  31.9 0.1 add_convert_fusion.refs_0_
  32.0 1.0 %finish.1 = bf16[4,4,64,256]{3,2,1,0:T(8,128)(2,1)} custom-call(s32[4]{0:T(128)S(1)} %copy-done, bf16[1,2,4,64,256]{4,3,2,1,0:T(8,128)(2,1)S(1)} %add_convert_fusion.refs_0_, bf16[1,1,4,64,256]{4,3,2,1,0:T(8,128)(2,1)S(1)} %add_convert_fusion.1.refs_1_, bf16[1,1,4,64,256]{4,3,2,1,0:T(8,128)(2,1)S(1)} %get-tuple-element.30.refs_2_, ...), custom_call_target="tpu_custom_call" | custom-call | tf_op jit(solution)/shard_map/finish/pallas_call | solution.py:186
  (14 shorter events, 0.1 us)
Async XLA Ops:
  0.0 7.0 %copy-start.3 = (s32[4,4]{1,0:T(4,128)S(1)}, s32[4,4]{1,0:T(4,128)}, u32[]{:S(2)}) copy-start(s32[4,4]{1,0:T(4,128)} %refs_0_.5) | copy-start | bytes 196
  0.0 7.0 %copy-start.2 = (f32[4,4,4]{2,1,0:T(4,128)S(1)}, f32[4,4,4]{2,1,0:T(4,128)}, u32[]{:S(2)}) copy-start(f32[4,4,4]{2,1,0:T(4,128)} %refs_1_.5) | copy-start | bytes 772
  0.0 7.0 %copy-start.1 = (bf16[4,4,256,256]{3,2,1,0:T(8,128)(2,1)S(1)}, bf16[4,4,256,256]{3,2,1,0:T(8,128)(2,1)}, u32[]{:S(2)}) copy-start(bf16[4,4,256,256]{3,2,1,0:T(8,128)(2,1)} %refs_2_.5) | copy-start | bytes 6291460
  1.9 5.0 %collective-permute-start = (bf16[1,4,256,256]{3,2,1,0:T(8,128)(2,1)S(1)}, bf16[1,4,256,256]{3,2,1,0:T(8,128)(2,1)S(1)}, u32[]{:S(2)}, u32[]{:S(2)}) collective-permute-start(bf16[1,4,256,256]{3,2,1,0:T(8,128)(2,1)S(1)} %get-tuple-element.19), channel_id=1, source_target_pairs={{0,4},{4,0},{8,12},{12,8},{16,20},{20,16},{24,28},{28,24},{1,5},{5... | collective-permute-start | bytes 1572872 | tf_op jit(solution)/shard_map/ppermute | solution.py:206
  2.4 4.5 %collective-permute-start.1 = (bf16[1,4,256,256]{3,2,1,0:T(8,128)(2,1)S(1)}, bf16[1,4,256,256]{3,2,1,0:T(8,128)(2,1)S(1)}, u32[]{:S(2)}, u32[]{:S(2)}) collective-permute-start(bf16[1,4,256,256]{3,2,1,0:T(8,128)(2,1)S(1)} %get-tuple-element.20), channel_id=1, source_target_pairs={{0,4},{4,0},{8,12},{12,8},{16,20},{20,16},{24,28},{28,24},{1,5},{5... | collective-permute-start | bytes 1572872 | tf_op jit(solution)/shard_map/ppermute | solution.py:206
  2.5 10.1 %collective-permute-start.4 = (bf16[1,4,256,256]{3,2,1,0:T(8,128)(2,1)S(1)}, bf16[1,4,256,256]{3,2,1,0:T(8,128)(2,1)S(1)}, u32[]{:S(2)}, u32[]{:S(2)}) collective-permute-start(bf16[1,4,256,256]{3,2,1,0:T(8,128)(2,1)S(1)} %get-tuple-element.23), channel_id=1, source_target_pairs={{0,1},{1,0},{2,3},{3,2},{4,8},{5,9},{6,10},{7,11},{8,4},{9,5},{10,... | collective-permute-start | bytes 1572872 | tf_op jit(solution)/shard_map/ppermute | solution.py:32
  5.4 11.5 %collective-permute-start.7 = (bf16[1,4,256,256]{3,2,1,0:T(8,128)(2,1)S(1)}, bf16[1,4,256,256]{3,2,1,0:T(8,128)(2,1)S(1)}, u32[]{:S(2)}, u32[]{:S(2)}) collective-permute-start(bf16[1,4,256,256]{3,2,1,0:T(8,128)(2,1)S(1)} %get-tuple-element.26), channel_id=1, source_target_pairs={{0,2},{1,3},{2,0},{3,1},{4,8},{5,9},{6,10},{7,11},{8,4},{9,5},{10,... | collective-permute-start | bytes 1572872 | tf_op jit(solution)/shard_map/ppermute | solution.py:32
  10.6 12.8 %collective-permute-start.2 = (bf16[2,2,4,64,256]{4,3,2,1,0:T(8,128)(2,1)S(1)}, bf16[2,2,4,64,256]{4,3,2,1,0:T(8,128)(2,1)S(1)}, u32[]{:S(2)}, u32[]{:S(2)}) collective-permute-start(bf16[2,2,4,64,256]{4,3,2,1,0:T(8,128)(2,1)S(1)} %get-tuple-element.22), channel_id=1, source_target_pairs={{0,1},{1,0},{2,3},{3,2},{4,6},{5,7},{6,4},{7,5},{8,9},{9,8},{10,11... | collective-permute-start | bytes 1572872 | tf_op jit(solution)/shard_map/ppermute | solution.py:21
  14.5 8.1 %collective-permute-start.5 = (bf16[2,1,4,64,256]{4,3,2,1,0:T(8,128)(2,1)S(1)}, bf16[2,1,4,64,256]{4,3,2,1,0:T(8,128)(2,1)S(1)}, u32[]{:S(2)}, u32[]{:S(2)}) collective-permute-start(bf16[2,1,4,64,256]{4,3,2,1,0:T(8,128)(2,1)S(1)} %get-tuple-element.25), channel_id=1, source_target_pairs={{0,1},{1,0},{2,3},{3,2},{4,6},{5,7},{6,4},{7,5},{8,9},{9,8},{10,11... | collective-permute-start | bytes 786440 | tf_op jit(solution)/shard_map/ppermute | solution.py:21
  18.9 13.1 %copy-start = (s32[4]{0:T(128)S(1)}, s32[4]{0:T(128)}, u32[]{:S(2)}) copy-start(s32[4]{0:T(128)} %live.1) | copy-start | bytes 52
  18.9 6.9 %collective-permute-start.8 = (bf16[2,1,4,64,256]{4,3,2,1,0:T(8,128)(2,1)S(1)}, bf16[2,1,4,64,256]{4,3,2,1,0:T(8,128)(2,1)S(1)}, u32[]{:S(2)}, u32[]{:S(2)}) collective-permute-start(bf16[2,1,4,64,256]{4,3,2,1,0:T(8,128)(2,1)S(1)} %get-tuple-element.28), channel_id=1, source_target_pairs={{0,2},{1,3},{2,0},{3,1},{4,5},{5,4},{6,7},{7,6},{8,10},{9,11},{10,... | collective-permute-start | bytes 786440 | tf_op jit(solution)/shard_map/ppermute | solution.py:21
  22.6 5.0 %collective-permute-start.6 = (bf16[1,1,4,64,256]{4,3,2,1,0:T(8,128)(2,1)S(1)}, bf16[1,1,4,64,256]{4,3,2,1,0:T(8,128)(2,1)S(1)}, u32[]{:S(2)}, u32[]{:S(2)}) collective-permute-start(bf16[1,1,4,64,256]{4,3,2,1,0:T(8,128)(2,1)S(1)} %slice_add_fusion.2), channel_id=1, source_target_pairs={{0,2},{1,3},{2,0},{3,1},{4,5},{5,4},{6,7},{7,6},{8,10},{9,11},{10,... | collective-permute-start | bytes 393224 | tf_op jit(solution)/shard_map/ppermute | solution.py:21
  23.4 8.5 %collective-permute-start.3 = (bf16[1,2,4,64,256]{4,3,2,1,0:T(8,128)(2,1)S(1)}, bf16[1,2,4,64,256]{4,3,2,1,0:T(8,128)(2,1)S(1)}, u32[]{:S(2)}, u32[]{:S(2)}) collective-permute-start(bf16[1,2,4,64,256]{4,3,2,1,0:T(8,128)(2,1)S(1)} %slice_add_fusion), channel_id=1, source_target_pairs={{0,2},{1,3},{2,0},{3,1},{4,5},{5,4},{6,7},{7,6},{8,10},{9,11},{10,... | collective-permute-start | bytes 786440 | tf_op jit(solution)/shard_map/ppermute | solution.py:21
  25.9 6.1 %collective-permute-start.9 = (bf16[1,1,4,64,256]{4,3,2,1,0:T(8,128)(2,1)S(1)}, bf16[1,1,4,64,256]{4,3,2,1,0:T(8,128)(2,1)S(1)}, u32[]{:S(2)}, u32[]{:S(2)}) collective-permute-start(bf16[1,1,4,64,256]{4,3,2,1,0:T(8,128)(2,1)S(1)} %get-tuple-element.29), channel_id=1, source_target_pairs={{0,1},{1,0},{2,3},{3,2},{4,6},{5,7},{6,4},{7,5},{8,9},{9,8},{10,11... | collective-permute-start | bytes 393224 | tf_op jit(solution)/shard_map/ppermute | solution.py:21

commit v4 on v3

--- a/solution.py
+++ b/solution.py
@@ -163,8 +163,7 @@
     col = lax.broadcasted_iota(jnp.int32, (rows, width), 1)
     copies = []
     for blocks in groups:
-        last = blocks is groups[-1]
-        terms, refs = (refs[:3], refs[3:]) if last else (refs[:1], refs[1:])
+        terms, refs = refs[:3], refs[3:]
         for n, block in enumerate(blocks):
             s = jnp.where(odd == 1, block[1], block[0])
             size = entry(live[...].reshape(1, own), 0, s)
@@ -226,10 +225,9 @@
             got = flip(send, routes, step)
         send = keep[1:] + got[1:]
         parts = [keep[:1], got[:1], flip(send, routes, len(bits) - 1)]
-        if g < len(groups) - 1:
-            sums.append(sum(v.astype(jnp.float32) for v in parts).astype(jnp.bfloat16))
+        sums += parts
     shape = (own, states, width // devices, width)
-    return finish(tuple(blocks for blocks, _ in groups), live, sums + parts, shape)
+    return finish(tuple(blocks for blocks, _ in groups), live, sums, shape)
 
 
 def solution(mesh):

time: 33.1 us -> 32.9 us (level)
  transfers between devices with their start and end apart: 10 -> 10, of which waited for: 6 -> 6; matrix products, arithmetic and copies ran while one was open for 1% -> 0% of each run, Pallas kernels for 23% -> 22%
where the time goes in v4:
time: 32.9 us; the launch traced here: 32.8 us
  starting transfers between devices  11.4 us (35%)
  waiting for transfers between devices  10.9 us (33%)
  Pallas kernels  10.3 us (31%)
    ppermute x6, waiting for transfers between devices, flip(): return lax.ppermute(value, ('sec', 'term'), pairs)  8.97 us
    pallas_call x3, Pallas kernels, apply_blocks(): pl.pallas_call(body, out_shape=[part] * 2, in_specs=[vmem] * (5 + len(ext...  7.35 us
    ppermute x6, starting transfers between devices, flip(): return lax.ppermute(value, ('sec', 'term'), pairs)  6.38 us
    ppermute x2, starting transfers between devices, over_link(): return lax.ppermute(value, ('sec', 'term'), pairs)  4.44 us
    ppermute x2, waiting for transfers between devices, over_link(): return lax.ppermute(value, ('sec', 'term'), pairs)  1.91 us
    pallas_call x1, Pallas kernels, pick(): pl.pallas_call(pick_body, out_shape=shapes, in_specs=[hbm, hbm], out_spec...  1.89 us
    pallas_call x1, Pallas kernels, finish(): pl.pallas_call(functools.partial(finish_body, groups), out_shape=pltpu.HB...  1 us
  transfers between devices with their start and end apart: 10, of which 6 were waited for; matrix products, arithmetic and copies ran while one was open for 0% of the time, Pallas kernels for 22%

profile of v4, /device:TPU:0, one launch (start us, length us, event | category | flops | bytes accessed | tf_op | source)
XLA Modules:
  0.0 32.8 jit_solution(3129996336809600349)
XLA Ops:
  0.0 1.9 %pick.1 = (bf16[4,4,256,256]{3,2,1,0:T(8,128)(2,1)S(1)}, bf16[4,256,256]{2,1,0:T(8,128)(2,1)S(1)}, bf16[1,4,256,256]{3,2,1,0:T(8,128)(2,1)S(1)}, bf16[1,4,256,25...) custom-call(bf16[4,4,256,256]{3,2,1,0:T(8,128)(2,1)} %psi.1, ...), custom_call_target="tpu_custom_call" | custom-call | tf_op jit(solution)/shard_map/pick/pallas_call | solution.py:53
  1.9 0.5 %collective-permute-start = (bf16[1,4,256,256]{3,2,1,0:T(8,128)(2,1)S(1)}, bf16[1,4,256,256]{3,2,1,0:T(8,128)(2,1)S(1)}, u32[]{:S(2)}, u32[]{:S(2)}) collective-permute-start(bf16[1,4,256,256]{3,2,1,0:T(8,128)(2,1)S(1)} %get-tuple-element.19), channel_id=1, source_target_pairs={{0,4},{4,0},{8,12},{12,8},{16,20},{20,16},{24,28},{28,24},{1,5},{5... | collective-permute-start | bytes 1572872 | tf_op jit(solution)/shard_map/ppermute | solution.py:205
  2.4 0.1 collective-permute-start.1
  2.5 2.9 %collective-permute-start.4 = (bf16[1,4,256,256]{3,2,1,0:T(8,128)(2,1)S(1)}, bf16[1,4,256,256]{3,2,1,0:T(8,128)(2,1)S(1)}, u32[]{:S(2)}, u32[]{:S(2)}) collective-permute-start(bf16[1,4,256,256]{3,2,1,0:T(8,128)(2,1)S(1)} %get-tuple-element.23), channel_id=1, source_target_pairs={{0,1},{1,0},{2,3},{3,2},{4,8},{5,9},{6,10},{7,11},{8,4},{9,5},{10,... | collective-permute-start | bytes 1572872 | tf_op jit(solution)/shard_map/ppermute | solution.py:32
  5.4 1.5 %collective-permute-start.7 = (bf16[1,4,256,256]{3,2,1,0:T(8,128)(2,1)S(1)}, bf16[1,4,256,256]{3,2,1,0:T(8,128)(2,1)S(1)}, u32[]{:S(2)}, u32[]{:S(2)}) collective-permute-start(bf16[1,4,256,256]{3,2,1,0:T(8,128)(2,1)S(1)} %get-tuple-element.26), channel_id=1, source_target_pairs={{0,2},{1,3},{2,0},{3,1},{4,8},{5,9},{6,10},{7,11},{8,4},{9,5},{10,... | collective-permute-start | bytes 1572872 | tf_op jit(solution)/shard_map/ppermute | solution.py:32
  7.0 3.4 %apply_2.1 = (bf16[2,2,4,64,256]{4,3,2,1,0:T(8,128)(2,1)S(1)}, bf16[2,2,4,64,256]{4,3,2,1,0:T(8,128)(2,1)S(1)}) custom-call(s32[4,4]{1,0:T(4,128)S(1)} %copy-done.3, f32[4,4,4]{2,1,0:T(4,128)S(1)} %copy-done.2, bf16[4,4,256,256]{3,2,1,0:T(8,128)(2,1)S(1)} %copy-done.1, bf16[4,256,256]{2,1,0:T(8,128)(2,1)S(1)} %get-tuple-element.17.refs_3_, ...), custom_call_target="tpu_custom_call" | custom-call | flops 21474836480 | bytes 8 | tf_op jit(solution)/shard_map/apply_2/pallas_call | solution.py:140
  10.4 0.7 %collective-permute-start.2 = (bf16[2,2,4,64,256]{4,3,2,1,0:T(8,128)(2,1)S(1)}, bf16[2,2,4,64,256]{4,3,2,1,0:T(8,128)(2,1)S(1)}, u32[]{:S(2)}, u32[]{:S(2)}) collective-permute-start(bf16[2,2,4,64,256]{4,3,2,1,0:T(8,128)(2,1)S(1)} %get-tuple-element.22), channel_id=1, source_target_pairs={{0,1},{1,0},{2,3},{3,2},{4,6},{5,7},{6,4},{7,5},{8,9},{9,8},{10,11... | collective-permute-start | bytes 1572872 | tf_op jit(solution)/shard_map/ppermute | solution.py:21
  11.1 1.5 %collective-permute-done.4.refs_5_ = bf16[1,4,256,256]{3,2,1,0:T(8,128)(2,1)S(1)} collective-permute-done((bf16[1,4,256,256]{3,2,1,0:T(8,128)(2,1)S(1)}, bf16[1,4,256,256]{3,2,1,0:T(8,128)(2,1)S(1)}, u32[]{:S(2)}, u32[]{:S(2)}) %collective-permute-start.4) | collective-permute-done | bytes 524320 | tf_op jit(solution)/shard_map/ppermute | solution.py:32
  12.6 1.9 %apply_1.1 = (bf16[2,1,4,64,256]{4,3,2,1,0:T(8,128)(2,1)S(1)}, bf16[2,1,4,64,256]{4,3,2,1,0:T(8,128)(2,1)S(1)}) custom-call(s32[4,4]{1,0:T(4,128)S(1)} %copy-done.3, f32[4,4,4]{2,1,0:T(4,128)S(1)} %copy-done.2, bf16[4,4,256,256]{3,2,1,0:T(8,128)(2,1)S(1)} %copy-done.1, bf16[4,256,256]{2,1,0:T(8,128)(2,1)S(1)} %get-tuple-element.17.refs_3_, ...), custom_call_target="tpu_custom_call" | custom-call | flops 10737418240 | bytes 4 | tf_op jit(solution)/shard_map/apply_1/pallas_call | solution.py:140
  14.5 2.1 %collective-permute-start.5 = (bf16[2,1,4,64,256]{4,3,2,1,0:T(8,128)(2,1)S(1)}, bf16[2,1,4,64,256]{4,3,2,1,0:T(8,128)(2,1)S(1)}, u32[]{:S(2)}, u32[]{:S(2)}) collective-permute-start(bf16[2,1,4,64,256]{4,3,2,1,0:T(8,128)(2,1)S(1)} %get-tuple-element.25), channel_id=1, source_target_pairs={{0,1},{1,0},{2,3},{3,2},{4,6},{5,7},{6,4},{7,5},{8,9},{9,8},{10,11... | collective-permute-start | bytes 786440 | tf_op jit(solution)/shard_map/ppermute | solution.py:21
  16.6 0.4 %collective-permute-done.7.refs_6_ = bf16[1,4,256,256]{3,2,1,0:T(8,128)(2,1)S(1)} collective-permute-done((bf16[1,4,256,256]{3,2,1,0:T(8,128)(2,1)S(1)}, bf16[1,4,256,256]{3,2,1,0:T(8,128)(2,1)S(1)}, u32[]{:S(2)}, u32[]{:S(2)}) %collective-permute-start.7) | collective-permute-done | bytes 524320 | tf_op jit(solution)/shard_map/ppermute | solution.py:32
  17.0 2.0 %apply_0.1 = (bf16[2,1,4,64,256]{4,3,2,1,0:T(8,128)(2,1)S(1)}, bf16[2,1,4,64,256]{4,3,2,1,0:T(8,128)(2,1)S(1)}) custom-call(s32[4,4]{1,0:T(4,128)S(1)} %copy-done.3, f32[4,4,4]{2,1,0:T(4,128)S(1)} %copy-done.2, bf16[4,4,256,256]{3,2,1,0:T(8,128)(2,1)S(1)} %copy-done.1, bf16[4,256,256]{2,1,0:T(8,128)(2,1)S(1)} %get-tuple-element.17.refs_3_, ...), custom_call_target="tpu_custom_call" | custom-call | flops 10737418240 | bytes 4 | tf_op jit(solution)/shard_map/apply_0/pallas_call | solution.py:140
  19.0 0.0 copy-start
  19.0 1.4 %collective-permute-start.8 = (bf16[2,1,4,64,256]{4,3,2,1,0:T(8,128)(2,1)S(1)}, bf16[2,1,4,64,256]{4,3,2,1,0:T(8,128)(2,1)S(1)}, u32[]{:S(2)}, u32[]{:S(2)}) collective-permute-start(bf16[2,1,4,64,256]{4,3,2,1,0:T(8,128)(2,1)S(1)} %get-tuple-element.28), channel_id=1, source_target_pairs={{0,2},{1,3},{2,0},{3,1},{4,5},{5,4},{6,7},{7,6},{8,10},{9,11},{10,... | collective-permute-start | bytes 786440 | tf_op jit(solution)/shard_map/ppermute | solution.py:21
  20.4 2.1 %collective-permute-done.5 = bf16[2,1,4,64,256]{4,3,2,1,0:T(8,128)(2,1)S(1)} collective-permute-done((bf16[2,1,4,64,256]{4,3,2,1,0:T(8,128)(2,1)S(1)}, bf16[2,1,4,64,256]{4,3,2,1,0:T(8,128)(2,1)S(1)}, u32[]{:S(2)}, u32[]{:S(2)}) %collective-permute-start.5) | collective-permute-done | bytes 262176 | tf_op jit(solution)/shard_map/ppermute | solution.py:21
  22.5 0.7 %collective-permute-start.6 = (bf16[1,1,4,64,256]{4,3,2,1,0:T(8,128)(2,1)S(1)}, bf16[1,1,4,64,256]{4,3,2,1,0:T(8,128)(2,1)S(1)}, u32[]{:S(2)}, u32[]{:S(2)}) collective-permute-start(bf16[1,1,4,64,256]{4,3,2,1,0:T(8,128)(2,1)S(1)} %get-tuple-element.35), channel_id=1, source_target_pairs={{0,2},{1,3},{2,0},{3,1},{4,5},{5,4},{6,7},{7,6},{8,10},{9,11},{10,... | collective-permute-start | bytes 393224 | tf_op jit(solution)/shard_map/ppermute | solution.py:21
  23.2 0.1 slice_add_fusion
  23.3 1.5 %collective-permute-start.3 = (bf16[1,2,4,64,256]{4,3,2,1,0:T(8,128)(2,1)S(1)}, bf16[1,2,4,64,256]{4,3,2,1,0:T(8,128)(2,1)S(1)}, u32[]{:S(2)}, u32[]{:S(2)}) collective-permute-start(bf16[1,2,4,64,256]{4,3,2,1,0:T(8,128)(2,1)S(1)} %get-tuple-element.29), channel_id=1, source_target_pairs={{0,2},{1,3},{2,0},{3,1},{4,5},{5,4},{6,7},{7,6},{8,10},{9,11},{10,... | collective-permute-start | bytes 786440 | tf_op jit(solution)/shard_map/ppermute | solution.py:21
  24.7 1.1 %collective-permute-done.8 = bf16[2,1,4,64,256]{4,3,2,1,0:T(8,128)(2,1)S(1)} collective-permute-done((bf16[2,1,4,64,256]{4,3,2,1,0:T(8,128)(2,1)S(1)}, bf16[2,1,4,64,256]{4,3,2,1,0:T(8,128)(2,1)S(1)}, u32[]{:S(2)}, u32[]{:S(2)}) %collective-permute-start.8) | collective-permute-done | bytes 262176 | tf_op jit(solution)/shard_map/ppermute | solution.py:21
  25.9 0.1 collective-permute-start.9
  26.0 1.6 %collective-permute-done.6.refs_5_ = bf16[1,1,4,64,256]{4,3,2,1,0:T(8,128)(2,1)S(1)} collective-permute-done((bf16[1,1,4,64,256]{4,3,2,1,0:T(8,128)(2,1)S(1)}, bf16[1,1,4,64,256]{4,3,2,1,0:T(8,128)(2,1)S(1)}, u32[]{:S(2)}, u32[]{:S(2)}) %collective-permute-start.6) | collective-permute-done | bytes 131104 | tf_op jit(solution)/shard_map/ppermute | solution.py:21
  27.6 4.2 %collective-permute-done.9.refs_8_ = bf16[1,1,4,64,256]{4,3,2,1,0:T(8,128)(2,1)S(1)} collective-permute-done((bf16[1,1,4,64,256]{4,3,2,1,0:T(8,128)(2,1)S(1)}, bf16[1,1,4,64,256]{4,3,2,1,0:T(8,128)(2,1)S(1)}, u32[]{:S(2)}, u32[]{:S(2)}) %collective-permute-start.9) | collective-permute-done | bytes 131104 | tf_op jit(solution)/shard_map/ppermute | solution.py:21
  31.8 0.0 collective-permute-done.3.refs_2_
  31.8 1.0 %finish.1 = bf16[4,4,64,256]{3,2,1,0:T(8,128)(2,1)} custom-call(s32[4]{0:T(128)S(1)} %copy-done, bf16[1,2,4,64,256]{4,3,2,1,0:T(8,128)(2,1)S(1)} %get-tuple-element.30.refs_0_, bf16[1,2,4,64,256]{4,3,2,1,0:T(8,128)(2,1)S(1)} %get-tuple-element.31.refs_1_, bf16[1,2,4,64,256]{4,3,2,1,0:T(8,128)(2,1)S(1)} %collective-permute-done.3.refs_2_, ...), custom_call_target="tpu_custom_call" | custom-call | tf_op jit(solution)/shard_map/finish/pallas_call | solution.py:185
  (12 shorter events, 0.1 us)
Async XLA Ops:
  0.0 7.0 %copy-start.3 = (s32[4,4]{1,0:T(4,128)S(1)}, s32[4,4]{1,0:T(4,128)}, u32[]{:S(2)}) copy-start(s32[4,4]{1,0:T(4,128)} %refs_0_.5) | copy-start | bytes 196
  0.0 7.0 %copy-start.2 = (f32[4,4,4]{2,1,0:T(4,128)S(1)}, f32[4,4,4]{2,1,0:T(4,128)}, u32[]{:S(2)}) copy-start(f32[4,4,4]{2,1,0:T(4,128)} %refs_1_.5) | copy-start | bytes 772
  0.0 7.0 %copy-start.1 = (bf16[4,4,256,256]{3,2,1,0:T(8,128)(2,1)S(1)}, bf16[4,4,256,256]{3,2,1,0:T(8,128)(2,1)}, u32[]{:S(2)}) copy-start(bf16[4,4,256,256]{3,2,1,0:T(8,128)(2,1)} %refs_2_.5) | copy-start | bytes 6291460
  1.9 5.0 %collective-permute-start = (bf16[1,4,256,256]{3,2,1,0:T(8,128)(2,1)S(1)}, bf16[1,4,256,256]{3,2,1,0:T(8,128)(2,1)S(1)}, u32[]{:S(2)}, u32[]{:S(2)}) collective-permute-start(bf16[1,4,256,256]{3,2,1,0:T(8,128)(2,1)S(1)} %get-tuple-element.19), channel_id=1, source_target_pairs={{0,4},{4,0},{8,12},{12,8},{16,20},{20,16},{24,28},{28,24},{1,5},{5... | collective-permute-start | bytes 1572872 | tf_op jit(solution)/shard_map/ppermute | solution.py:205
  2.4 4.5 %collective-permute-start.1 = (bf16[1,4,256,256]{3,2,1,0:T(8,128)(2,1)S(1)}, bf16[1,4,256,256]{3,2,1,0:T(8,128)(2,1)S(1)}, u32[]{:S(2)}, u32[]{:S(2)}) collective-permute-start(bf16[1,4,256,256]{3,2,1,0:T(8,128)(2,1)S(1)} %get-tuple-element.20), channel_id=1, source_target_pairs={{0,4},{4,0},{8,12},{12,8},{16,20},{20,16},{24,28},{28,24},{1,5},{5... | collective-permute-start | bytes 1572872 | tf_op jit(solution)/shard_map/ppermute | solution.py:205
  2.5 10.1 %collective-permute-start.4 = (bf16[1,4,256,256]{3,2,1,0:T(8,128)(2,1)S(1)}, bf16[1,4,256,256]{3,2,1,0:T(8,128)(2,1)S(1)}, u32[]{:S(2)}, u32[]{:S(2)}) collective-permute-start(bf16[1,4,256,256]{3,2,1,0:T(8,128)(2,1)S(1)} %get-tuple-element.23), channel_id=1, source_target_pairs={{0,1},{1,0},{2,3},{3,2},{4,8},{5,9},{6,10},{7,11},{8,4},{9,5},{10,... | collective-permute-start | bytes 1572872 | tf_op jit(solution)/shard_map/ppermute | solution.py:32
  5.4 11.6 %collective-permute-start.7 = (bf16[1,4,256,256]{3,2,1,0:T(8,128)(2,1)S(1)}, bf16[1,4,256,256]{3,2,1,0:T(8,128)(2,1)S(1)}, u32[]{:S(2)}, u32[]{:S(2)}) collective-permute-start(bf16[1,4,256,256]{3,2,1,0:T(8,128)(2,1)S(1)} %get-tuple-element.26), channel_id=1, source_target_pairs={{0,2},{1,3},{2,0},{3,1},{4,8},{5,9},{6,10},{7,11},{8,4},{9,5},{10,... | collective-permute-start | bytes 1572872 | tf_op jit(solution)/shard_map/ppermute | solution.py:32
  10.4 12.8 %collective-permute-start.2 = (bf16[2,2,4,64,256]{4,3,2,1,0:T(8,128)(2,1)S(1)}, bf16[2,2,4,64,256]{4,3,2,1,0:T(8,128)(2,1)S(1)}, u32[]{:S(2)}, u32[]{:S(2)}) collective-permute-start(bf16[2,2,4,64,256]{4,3,2,1,0:T(8,128)(2,1)S(1)} %get-tuple-element.22), channel_id=1, source_target_pairs={{0,1},{1,0},{2,3},{3,2},{4,6},{5,7},{6,4},{7,5},{8,9},{9,8},{10,11... | collective-permute-start | bytes 1572872 | tf_op jit(solution)/shard_map/ppermute | solution.py:21
  14.5 8.0 %collective-permute-start.5 = (bf16[2,1,4,64,256]{4,3,2,1,0:T(8,128)(2,1)S(1)}, bf16[2,1,4,64,256]{4,3,2,1,0:T(8,128)(2,1)S(1)}, u32[]{:S(2)}, u32[]{:S(2)}) collective-permute-start(bf16[2,1,4,64,256]{4,3,2,1,0:T(8,128)(2,1)S(1)} %get-tuple-element.25), channel_id=1, source_target_pairs={{0,1},{1,0},{2,3},{3,2},{4,6},{5,7},{6,4},{7,5},{8,9},{9,8},{10,11... | collective-permute-start | bytes 786440 | tf_op jit(solution)/shard_map/ppermute | solution.py:21
  19.0 12.7 %copy-start = (s32[4]{0:T(128)S(1)}, s32[4]{0:T(128)}, u32[]{:S(2)}) copy-start(s32[4]{0:T(128)} %live.1) | copy-start | bytes 52
  19.0 6.8 %collective-permute-start.8 = (bf16[2,1,4,64,256]{4,3,2,1,0:T(8,128)(2,1)S(1)}, bf16[2,1,4,64,256]{4,3,2,1,0:T(8,128)(2,1)S(1)}, u32[]{:S(2)}, u32[]{:S(2)}) collective-permute-start(bf16[2,1,4,64,256]{4,3,2,1,0:T(8,128)(2,1)S(1)} %get-tuple-element.28), channel_id=1, source_target_pairs={{0,2},{1,3},{2,0},{3,1},{4,5},{5,4},{6,7},{7,6},{8,10},{9,11},{10,... | collective-permute-start | bytes 786440 | tf_op jit(solution)/shard_map/ppermute | solution.py:21
  22.5 5.0 %collective-permute-start.6 = (bf16[1,1,4,64,256]{4,3,2,1,0:T(8,128)(2,1)S(1)}, bf16[1,1,4,64,256]{4,3,2,1,0:T(8,128)(2,1)S(1)}, u32[]{:S(2)}, u32[]{:S(2)}) collective-permute-start(bf16[1,1,4,64,256]{4,3,2,1,0:T(8,128)(2,1)S(1)} %get-tuple-element.35), channel_id=1, source_target_pairs={{0,2},{1,3},{2,0},{3,1},{4,5},{5,4},{6,7},{7,6},{8,10},{9,11},{10,... | collective-permute-start | bytes 393224 | tf_op jit(solution)/shard_map/ppermute | solution.py:21
  23.3 8.5 %collective-permute-start.3 = (bf16[1,2,4,64,256]{4,3,2,1,0:T(8,128)(2,1)S(1)}, bf16[1,2,4,64,256]{4,3,2,1,0:T(8,128)(2,1)S(1)}, u32[]{:S(2)}, u32[]{:S(2)}) collective-permute-start(bf16[1,2,4,64,256]{4,3,2,1,0:T(8,128)(2,1)S(1)} %get-tuple-element.29), channel_id=1, source_target_pairs={{0,2},{1,3},{2,0},{3,1},{4,5},{5,4},{6,7},{7,6},{8,10},{9,11},{10,... | collective-permute-start | bytes 786440 | tf_op jit(solution)/shard_map/ppermute | solution.py:21
  25.9 5.9 %collective-permute-start.9 = (bf16[1,1,4,64,256]{4,3,2,1,0:T(8,128)(2,1)S(1)}, bf16[1,1,4,64,256]{4,3,2,1,0:T(8,128)(2,1)S(1)}, u32[]{:S(2)}, u32[]{:S(2)}) collective-permute-start(bf16[1,1,4,64,256]{4,3,2,1,0:T(8,128)(2,1)S(1)} %get-tuple-element.32), channel_id=1, source_target_pairs={{0,1},{1,0},{2,3},{3,2},{4,6},{5,7},{6,4},{7,5},{8,9},{9,8},{10,11... | collective-permute-start | bytes 393224 | tf_op jit(solution)/shard_map/ppermute | solution.py:21
